TPU v7x, 512 devices: a whole 4x8x8 slice. The times are simulated.
512 devices in a mesh: rep: 16 (over y_lo, z), tok: 32 (over x, y_hi, core).
Axes of the slice: x: 4, y: 8 (y_hi: 4, y_lo: 2; y = y_hi * 2 + y_lo), z: 8, core: 2. Of those that a mesh axis runs over, the one named last changes fastest.
Arguments:
- query_rows: bfloat16 [16, 4096, 1024], P('rep', 'tok'), may hold values from -144 to 144
- key_rows: bfloat16 [16, 4096, 1024], P('rep', 'tok'), may hold values from -7 to 7
- value_rows: bfloat16 [16, 4096, 1024], P('rep', 'tok'), may hold values from -6 to 6
- cotangent: bfloat16 [16, 4096, 1024], P('rep', 'tok'), may hold values from -6 to 6
- out_weight: bfloat16 [1024, 1024], replicated, may hold values from -0.1875 to 0.1875
- error_rows: float32 [16, 1024, 1024], P('rep', 'tok'), may hold values from -4 to 4
- window_shift: int32 [16], P('rep'), may hold values from 0 to 127
- basis_seed: int32 [1], replicated, may hold values from 0 to 999
Outputs:
- projected: bfloat16 [16, 4096, 1024], P('rep', 'tok')
- query_grad: bfloat16 [16, 4096, 1024], P('rep', 'tok')
- key_grad: bfloat16 [16, 4096, 1024], P('rep', 'tok')
- value_grad: bfloat16 [16, 4096, 1024], P('rep', 'tok')
- weight_update: float32 [1024, 1024], P('tok')
- new_error: float32 [16, 1024, 1024], P('rep', 'tok')
- new_basis: float32 [1024, 32], replicated
All inputs are finite; a program needn't handle non-finite values.
Results may differ from a plain program's by a relative error of at most 0.007.
Values may be sent and summed in bfloat16 or wider, within the bound.
A program may use at most 128 MiB of HBM per device.

v0:
```python
import math

import jax
import jax.numpy as jnp
from jax import lax
from jax.sharding import PartitionSpec as P

H = 16
HD = 64
WIN = 128
RANK = 32


def padded_2(cells, sides, width):
    for axis, dim in sides:
        count = lax.axis_size(axis)
        head = lax.slice_in_dim(cells, 0, width, axis=dim)
        tail = lax.slice_in_dim(cells, cells.shape[dim] - width, cells.shape[dim], axis=dim)
        cells = jnp.concatenate(
            [
                lax.ppermute(tail, axis, [(i, (i + 1) % count) for i in range(count)]),
                cells,
                lax.ppermute(head, axis, [((i + 1) % count, i) for i in range(count)]),
            ],
            axis=dim,
        )
    return cells


def seeded_basis(seed_value, row_count, col_count):
    row_index = jnp.arange(row_count, dtype=jnp.int32)[:, None]
    col_index = jnp.arange(col_count, dtype=jnp.int32)[None, :]
    mixed = (row_index * 7919 + col_index * 31337 + seed_value * 17 + 12345) % 65521
    mixed = (mixed * 3877 + 29) % 65521
    mixed = (mixed * 2011 + 7) % 65521
    return mixed.astype(jnp.float32) / 65521.0 - 0.5


def body(
    query_rows, key_rows, value_rows, cotangent, out_weight, error_rows, window_shift, basis_seed
):
    query = query_rows[0]
    upstream = cotangent[0]
    rows_dev, width = query.shape
    tok_count = lax.axis_size("tok")
    rep_count = lax.axis_size("rep")
    position = lax.axis_index("tok")
    shift = window_shift[0]
    total = rows_dev * tok_count
    scale_factor = 1.0 / math.sqrt(HD)
    highest = lax.Precision.HIGHEST
    stacked = jnp.stack([key_rows[0], value_rows[0]], 0)
    padded = padded_2(stacked, (("tok", 1),), WIN)
    query_pos = position * rows_dev + jnp.arange(rows_dev, dtype=jnp.int32)
    key_pos = (position * rows_dev - WIN + jnp.arange(rows_dev + 2 * WIN, dtype=jnp.int32)) % total
    query_window = (query_pos - shift) % total // WIN
    key_window = (key_pos - shift) % total // WIN
    dattn = lax.dot_general(
        upstream, out_weight, (((1,), (1,)), ((), ())), preferred_element_type=jnp.float32
    ).astype(jnp.bfloat16)
    query_heads = query.reshape(rows_dev, H, HD)
    dattn_heads = dattn.reshape(rows_dev, H, HD)
    block_rows = min(rows_dev, 256)
    span = block_rows + 2 * WIN
    pad_grad = jnp.zeros((2, rows_dev + 2 * WIN, width), jnp.float32)
    key_blk = padded[0, 0:span].reshape(span, H, HD)
    value_blk = padded[1, 0:span].reshape(span, H, HD)
    scores = (
        jnp.einsum("qhd,khd->hqk", query_heads, key_blk, preferred_element_type=jnp.float32)
        * scale_factor
    )
    visible = query_window[:, None] == key_window[None, :]
    scores = jnp.where(visible[None], scores, -1e30)
    top = jnp.max(scores, axis=-1, keepdims=True)
    expo = jnp.exp(scores - top)
    probs = expo / jnp.sum(expo, axis=-1, keepdims=True)
    probs_low = probs.astype(jnp.bfloat16)
    attn_blk = jnp.einsum("hqk,khd->qhd", probs_low, value_blk, preferred_element_type=jnp.float32)
    attn_parts = attn_blk.astype(jnp.bfloat16).reshape(block_rows, width)
    dprob = jnp.einsum("qhd,khd->hqk", dattn_heads, value_blk, preferred_element_type=jnp.float32)
    delta = jnp.sum(probs * dprob, axis=-1, keepdims=True)
    dscore = (probs * (dprob - delta) * scale_factor).astype(jnp.bfloat16)
    qgrad_blk = jnp.einsum("hqk,khd->qhd", dscore, key_blk, preferred_element_type=jnp.float32)
    qgrad_parts = qgrad_blk.astype(jnp.bfloat16).reshape(block_rows, width)
    kgrad_part = jnp.einsum(
        "hqk,qhd->khd", dscore, query_heads, preferred_element_type=jnp.float32
    ).reshape(span, width)
    vgrad_part = jnp.einsum(
        "hqk,qhd->khd", probs_low, dattn_heads, preferred_element_type=jnp.float32
    ).reshape(span, width)
    pad_grad = pad_grad.at[:, 0:span].add(jnp.stack([kgrad_part, vgrad_part], 0))
    owed = jnp.concatenate([pad_grad[:, :WIN], pad_grad[:, -WIN:]], 1)
    received = padded_2(owed, (("tok", 1),), WIN)
    own_grad = pad_grad[:, WIN : WIN + rows_dev]
    own_grad = own_grad.at[:, :WIN].add(received[:, :WIN])
    own_grad = own_grad.at[:, rows_dev - WIN :].add(received[:, -WIN:])
    key_grad = own_grad[0].astype(jnp.bfloat16)
    value_grad = own_grad[1].astype(jnp.bfloat16)
    projected = jnp.dot(attn_parts, out_weight, preferred_element_type=jnp.float32).astype(
        jnp.bfloat16
    )
    row_count = width // tok_count
    slabs = lax.all_to_all(attn_parts, "tok", split_axis=1, concat_axis=0, tiled=True)
    grad_rows = lax.dot_general(
        slabs,
        lax.all_gather(upstream, "tok", axis=0, tiled=True),
        (((0,), (0,)), ((), ())),
        preferred_element_type=jnp.float32,
    )
    merged = grad_rows * (1.0 / math.sqrt(total)) + error_rows[0]
    basis = seeded_basis(basis_seed[0], width, RANK)
    left_rows = jnp.dot(merged, basis, precision=highest)
    whole = lax.dynamic_update_slice_in_dim(
        jnp.zeros((width, RANK), jnp.float32), left_rows, position * row_count, 0
    )
    whole = lax.psum(whole, ("rep", "tok")) / rep_count
    gram = jnp.dot(whole.T, whole, precision=highest)
    left_mine = lax.dynamic_slice_in_dim(whole, position * row_count, row_count, 0)
    lower = jnp.linalg.cholesky(gram)
    ortho = lax.linalg.triangular_solve(
        lower, left_mine, left_side=False, lower=True, transpose_a=True
    )
    partial_basis = lax.dot_general(merged, ortho, (((0,), (0,)), ((), ())), precision=highest)
    new_basis = lax.psum(partial_basis, ("rep", "tok")) / rep_count
    weight_update = jnp.dot(ortho, new_basis.T, precision=highest)
    new_error = (merged - weight_update)[None]
    return (
        projected[None],
        qgrad_parts[None],
        key_grad[None],
        value_grad[None],
        weight_update,
        new_error,
        new_basis,
    )


def solution(mesh):
    return jax.shard_map(
        body,
        mesh=mesh,
        in_specs=(
            P("rep", "tok", None),
            P("rep", "tok", None),
            P("rep", "tok", None),
            P("rep", "tok", None),
            P(),
            P("rep", "tok", None),
            P("rep"),
            P(),
        ),
        out_specs=(
            P("rep", "tok", None),
            P("rep", "tok", None),
            P("rep", "tok", None),
            P("rep", "tok", None),
            P("tok", None),
            P("rep", "tok", None),
            P(),
        ),
        check_vma=False,
    )
```

profile of v0, /device:TPU:1, one launch (start us, length us, event | category | flops | bytes accessed | tf_op | source)
XLA Modules:
  0.0 662.1 jit_solution(5980637194454181509)
XLA Ops:
  7.2 0.7 all-gather.3.cloned.1.call-update
  7.9 1.0 constant_dynamic-update-slice_fusion.1
  8.9 1.0 constant_dynamic-update-slice_fusion
  9.9 8.8 %collective-permute-start.1 = (bf16[2,128,1024]{2,1,0:T(8,128)(2,1)S(1)}, bf16[2,128,1024]{2,1,0:T(8,128)(2,1)}, u32[]{:S(2)}, u32[]{:S(2)}) collective-permute-start(bf16[2,128,1024]{2,1,0:T(8,128)(2,1)S(1)} %constant_dynamic-update-slice_fusion), channel_id=1, source_target_pairs={{1,0},{2,1},{3,2},{4,3},{5,4},{6,5},{7,6},{8,7},{9,8},{10,9},{11,1... | collective-permute-start | bytes 1572872 | tf_op jit(solution)/shard_map/ppermute | solution.py:23
  18.7 1.9 collective-permute-start
  21.2 1.1 copy.48
  22.4 1.8 convolution_convert_fusion
  25.2 3.2 collective-permute-done.1
  28.4 3.7 collective-permute-done
  32.1 1.3 pad_maximum_fusion
  33.4 1.4 fusion.104
  34.8 1.5 copy.46
  36.3 2.3 copy.47
  38.6 2.4 fusion.107
  41.0 4.1 fusion.106
  45.1 7.0 %fusion.9 = f32[16,384,64]{1,2,0:T(8,128)} fusion(bf16[128,16,64]{0,2,1:T(8,128)(2,1)S(1)} %bitcast.93, f32[16,128,384]{1,2,0:T(8,128)} %fusion.107, f32[16,128,384]{1,2,0:T(8,128)} %get-tuple-element.95, f32[16,128]{1,0:T(8,128)S(1)} %get-tuple-element.94), kind=kOutput, calls=%fused_computation.14 | convolution fusion | flops 106170752 | bytes 8134656 | tf_op jit(solution)/shard_map/hqk,qhd->khd/dot_general | solution.py:85
  52.0 3.0 copy.56
  55.1 3.9 fusion.34
  59.0 3.0 copy.57
  62.0 3.1 convolution_convert_fusion.2
  65.1 10.6 %all-to-all-start = ((bf16[128,32,32]{0,2,1:T(8,128)(2,1)}), bf16[128,32,32]{0,2,1:T(8,128)(2,1)S(1)}, u32[]{:S(2)}, u32[]{:S(2)}) async-start(bf16[128,32,32]{0,2,1:T(8,128)(2,1)} %bitcast.16), calls=%async_computation | async-start | bytes 524288 | tf_op jit(solution)/shard_map/all_to_all | solution.py:103
  75.8 3.1 fusion.29
  78.9 2.4 collective-permute-start.3
  81.3 4.0 collective-permute-start.2
  85.4 6.1 fusion.19
  91.5 0.9 copy.60
  92.4 2.1 fusion.22
  94.5 1.0 all-to-all-done
  95.5 11.4 %all-gather.3.cloned.1.call-done = bf16[1,4096,1024]{2,1,0:T(8,128)(2,1)} async-done(((bf16[1,128,1024]{2,1,0:T(8,128)(2,1)}), bf16[1,4096,1024]{2,1,0:T(8,128)(2,1)}) %all-gather.3.cloned.1.call-update) | async-done | bytes 8388624 | tf_op jit(solution)/shard_map/all_gather | solution.py:106
  106.9 4.9 fusion.26
  111.8 1.8 fusion.46
  113.7 0.4 dynamic_update_slice.3
  114.1 0.6 copy-done.4
  114.9 1.8 collective-permute-done.2
  116.7 2.1 fusion.33
  118.8 269.3 %all-reduce.3.cloned.1.call-done = f32[1024,32]{0,1:T(8,128)} async-done(((f32[1024,32]{0,1:T(8,128)}), f32[1024,32]{0,1:T(8,128)}) %all-reduce.3.cloned.1.call-update) | async-done | bytes 131088 | tf_op jit(solution)/shard_map/psum | solution.py:116
  388.1 1.2 fusion.103
  389.4 2.9 cholesky.16
  392.4 0.6 compare_reduce_fusion
  393.0 0.7 fusion.76
  393.7 2.4 custom-call.6
  396.1 0.9 broadcast_multiply_fusion.1
  397.1 0.3 fusion.77
  397.3 1.0 fusion.108
  398.3 0.8 fusion.105
  399.2 254.5 %all-reduce.5.cloned.1.call-done = f32[1024,32]{0,1:T(8,128)} async-done(((f32[1024,32]{0,1:T(8,128)}), f32[1024,32]{0,1:T(8,128)}) %all-reduce.5.cloned.1.call-update) | async-done | bytes 131088 | tf_op jit(solution)/shard_map/psum | solution.py:124
  653.6 0.9 broadcast_multiply_fusion
  654.8 0.7 subtract_bitcast_fusion
  (28 shorter events, 0.9 us)
Async XLA Ops:
  7.2 15.2 %copy-start = (bf16[1024,1024]{1,0:T(8,128)(2,1)S(1)}, bf16[1024,1024]{1,0:T(8,128)(2,1)}, u32[]{:S(2)}) copy-start(bf16[1024,1024]{1,0:T(8,128)(2,1)} %param.24) | copy-start | bytes 6291460
  7.2 99.7 %all-gather.3.cloned.1.call-start = ((), (), s32[]{:S(2)}) async-start(), calls=%async_computation.3 | async-start | bytes 8650752 | tf_op jit(solution)/shard_map/all_gather | solution.py:106
  9.9 18.5 %collective-permute-start.1 = (bf16[2,128,1024]{2,1,0:T(8,128)(2,1)S(1)}, bf16[2,128,1024]{2,1,0:T(8,128)(2,1)}, u32[]{:S(2)}, u32[]{:S(2)}) collective-permute-start(bf16[2,128,1024]{2,1,0:T(8,128)(2,1)S(1)} %constant_dynamic-update-slice_fusion), channel_id=1, source_target_pairs={{1,0},{2,1},{3,2},{4,3},{5,4},{6,5},{7,6},{8,7},{9,8},{10,9},{11,1... | collective-permute-start | bytes 1572872 | tf_op jit(solution)/shard_map/ppermute | solution.py:23
  18.7 13.4 %collective-permute-start = (bf16[2,128,1024]{2,1,0:T(8,128)(2,1)S(1)}, bf16[2,128,1024]{2,1,0:T(8,128)(2,1)}, u32[]{:S(2)}, u32[]{:S(2)}) collective-permute-start(bf16[2,128,1024]{2,1,0:T(8,128)(2,1)S(1)} %constant_dynamic-update-slice_fusion), channel_id=1, source_target_pairs={{0,1},{1,2},{2,3},{3,4},{4,5},{5,6},{6,7},{7,8},{8,9},{9,10},{10,1... | collective-permute-start | bytes 1572872 | tf_op jit(solution)/shard_map/ppermute | solution.py:21
  65.1 20.3 %copy-start.1 = (bf16[1,384,1024]{1,2,0:T(8,128)(2,1)S(1)}, bf16[1,384,1024]{1,2,0:T(8,128)(2,1)}, u32[]{:S(2)}) copy-start(bf16[1,384,1024]{1,2,0:T(8,128)(2,1)} %copy.47) | copy-start | bytes 2359300
  65.1 30.4 %all-to-all-start = ((bf16[128,32,32]{0,2,1:T(8,128)(2,1)}), bf16[128,32,32]{0,2,1:T(8,128)(2,1)S(1)}, u32[]{:S(2)}, u32[]{:S(2)}) async-start(bf16[128,32,32]{0,2,1:T(8,128)(2,1)} %bitcast.16), calls=%async_computation | async-start | bytes 524288 | tf_op jit(solution)/shard_map/all_to_all | solution.py:103
  75.7 312.4 %all-reduce.3.cloned.1.call-start = ((), (), s32[]{:S(2)}) async-start(), calls=%async_computation.1 | async-start | bytes 262144 | tf_op jit(solution)/shard_map/psum | solution.py:116
  78.9 35.9 %collective-permute-start.3 = (f32[2,128,1024]{2,1,0:T(8,128)}, f32[2,128,1024]{2,1,0:T(8,128)}, u32[]{:S(2)}, u32[]{:S(2)}) collective-permute-start(f32[2,128,1024]{2,1,0:T(8,128)} %get-tuple-element.89), channel_id=1, source_target_pairs={{1,0},{2,1},{3,2},{4,3},{5,4},{6,5},{7,6},{8,7},{9,8},{10,9},{11,1... | collective-permute-start | bytes 3145736 | tf_op jit(solution)/shard_map/ppermute | solution.py:23
  81.3 35.4 %collective-permute-start.2 = (f32[2,128,1024]{2,1,0:T(8,128)}, f32[2,128,1024]{2,1,0:T(8,128)}, u32[]{:S(2)}, u32[]{:S(2)}) collective-permute-start(f32[2,128,1024]{2,1,0:T(8,128)} %get-tuple-element.88), channel_id=1, source_target_pairs={{0,1},{1,2},{2,3},{3,4},{4,5},{5,6},{6,7},{7,8},{8,9},{9,10},{10,1... | collective-permute-start | bytes 3145736 | tf_op jit(solution)/shard_map/ppermute | solution.py:21
  91.5 15.4 %copy-start.5 = (f32[1,32,1024]{2,1,0:T(8,128)S(1)}, f32[1,32,1024]{2,1,0:T(8,128)}, u32[]{:S(2)}) copy-start(f32[1,32,1024]{2,1,0:T(8,128)} %param.25) | copy-start | bytes 393220
  114.1 0.7 copy-start.4
  114.8 538.8 %all-reduce.5.cloned.1.call-start = ((), (), s32[]{:S(2)}) async-start(), calls=%async_computation.2 | async-start | bytes 262144 | tf_op jit(solution)/shard_map/psum | solution.py:124
  654.5 1.0 copy-start.3
  654.8 0.7 copy-start.2
Sparse Core Ops, SparseCore 0:
  11.2 95.6 all-gather.2
  114.9 273.1 all-reduce.2
  398.5 255.1 all-reduce.4
where the time goes:
time: 663 us; the launch traced here: 662 us
  waiting for transfers between devices  546 us (82%)
  matrix products  39.9 us (6%)
  starting transfers between devices  27.9 us (4%)
  local copies, waits for them, and re-layouts  17.4 us (3%)
  other arithmetic  15.9 us (2%)
  between operations  15.3 us (2%)
    psum x1, waiting for transfers between devices, body(): whole = lax.psum(whole, ('rep', 'tok')) / rep_count  269 us
    psum x1, waiting for transfers between devices, body(): new_basis = lax.psum(partial_basis, ('rep', 'tok')) / rep_count  254 us
  transfers between devices with their start and end apart: 8, of which 7 were waited for; matrix products, arithmetic and copies ran while one was open for 9% of the time, Pallas kernels for 0%

commit v1 on v0

v1 whole, which is shorter than its diff:
```python
import math

import jax
import jax.numpy as jnp
from jax import lax
from jax.experimental import pallas as pl
from jax.experimental.pallas import tpu as pltpu
from jax.sharding import PartitionSpec as P

H = 16
HD = 64
WIN = 128
HALF = 64
RANK = 32
WIDTH = 1024
TOK = 32
REP = 16
GRAD_SCALE = 1.0 / 64.0
F32 = jnp.float32
BF16 = jnp.bfloat16
MESH = pl.DeviceIdType.MESH
HIGHEST = lax.Precision.HIGHEST
NN = (((1,), (0,)), ((), ()))
NT = (((1,), (1,)), ((), ()))
TN = (((0,), (0,)), ((), ()))


def seeded_basis_t(seed_value):
    row_index = jnp.arange(WIDTH, dtype=jnp.int32)[None, :]
    col_index = jnp.arange(RANK, dtype=jnp.int32)[:, None]
    mixed = (row_index * 7919 + col_index * 31337 + seed_value * 17 + 12345) % 65521
    mixed = (mixed * 3877 + 29) % 65521
    mixed = (mixed * 2011 + 7) % 65521
    return mixed.astype(F32) / 65521.0 - 0.5


def mm(a, b, dims=NN):
    return lax.dot_general(a, b, dims, preferred_element_type=F32)


def mm_exact(a, b, dims=NN):
    return lax.dot_general(a, b, dims, precision=HIGHEST, preferred_element_type=F32)


def mm_split(a, b, dims=NN):
    high = a.astype(BF16)
    rest = a - high.astype(F32)
    middle = rest.astype(BF16)
    low = (rest - middle.astype(F32)).astype(BF16)
    out = mm(jnp.concatenate([high, middle, low], 0), b, dims)
    return (out[2 * RANK :] + out[RANK : 2 * RANK]) + out[:RANK]


def one_hot(shape, row_to_col):
    rows = lax.broadcasted_iota(jnp.int32, shape, 0)
    cols = lax.broadcasted_iota(jnp.int32, shape, 1)
    return jnp.where(row_to_col(rows, cols), 1.0, 0.0).astype(BF16)


def to_tiles(ref, field):
    for i in range(4):
        for j in range(8):
            ref[i * 8 + j] = field[i * 8 : i * 8 + 8, j * 128 : j * 128 + 128]


def attend_kernel(
    shift, query, key, value, cot, weight, basis, error,
    outs, grad, left, attn_out, cot_out,
    cat, weight_v, win, dattn, proj, send_sem, recv_sem, local_sem,
):
    me = lax.axis_index("tok")
    next_dev, prev_dev = lax.rem(me + 1, TOK), lax.rem(me + TOK - 1, TOK)
    barrier = pltpu.get_barrier_semaphore()
    for dev in (next_dev, prev_dev):
        pl.semaphore_signal(barrier, inc=1, device_id={"tok": dev}, device_id_type=MESH)
    local = []
    sources = (cot, key, query, value)
    for i, src in enumerate(sources):
        local.append(pltpu.make_async_copy(src, cat.at[i, pl.ds(HALF, WIN)], local_sem.at[i]))
    local.append(pltpu.make_async_copy(weight, weight_v, local_sem.at[4]))
    for copy in local:
        copy.start()
    pl.semaphore_wait(barrier, 2)
    halo = []
    for i, src in enumerate(sources):
        halo.append(
            pltpu.make_async_remote_copy(
                src.at[pl.ds(0, HALF)], cat.at[i, pl.ds(HALF + WIN, HALF)],
                send_sem.at[2 * i], recv_sem.at[2 * i],
                device_id={"tok": prev_dev}, device_id_type=MESH,
            )
        )
        halo.append(
            pltpu.make_async_remote_copy(
                src.at[pl.ds(HALF, HALF)], cat.at[i, pl.ds(0, HALF)],
                send_sem.at[2 * i + 1], recv_sem.at[2 * i + 1],
                device_id={"tok": next_dev}, device_id_type=MESH,
            )
        )
    for copy in halo:
        copy.start()
    for copy in local:
        copy.wait()

    offset = shift[0]
    start = jnp.where(offset <= HALF, offset + HALF, offset - HALF)
    pick = one_hot((WIN, 2 * WIN), lambda r, c: c == r + start)
    place = one_hot((2 * WIN, WIN), lambda r, c: r == c + start)
    head = lax.broadcasted_iota(jnp.int32, (WIN, 4 * HD), 1) // HD
    masks = [jnp.where(head == h, 1.0, 0.0).astype(BF16) for h in range(4)]

    for i in range(4):
        halo[2 * i].wait_recv()
        halo[2 * i + 1].wait_recv()
        win[i] = mm(pick, cat[i]).astype(BF16)
        if i == 0:
            cot_out[...] = win[0]
            dattn[...] = mm(win[0], weight_v[...], NT).astype(BF16)

    def spread(x):
        return jnp.concatenate([x * mask for mask in masks], 0)

    def lanes(x):
        return jnp.concatenate([x[h] for h in range(4)], 1)

    for g in range(4):
        cols = slice(g * 256, g * 256 + 256)
        k4, q4, v4, d4 = win[1, :, cols], win[2, :, cols], win[3, :, cols], dattn[:, cols]
        kbd, qbd, vbd, dbd = spread(k4), spread(q4), spread(v4), spread(d4)
        scores = (mm(kbd, q4, NT) * 0.125).reshape(4, WIN, WIN)
        expo = jnp.exp(scores - jnp.max(scores, axis=1, keepdims=True))
        probs = expo / jnp.sum(expo, axis=1, keepdims=True)
        low = probs.astype(BF16)
        dprob = mm(vbd, d4, NT).reshape(4, WIN, WIN)
        delta = jnp.sum(probs * dprob, axis=1, keepdims=True)
        dscore = (probs * (dprob - delta) * 0.125).astype(BF16)
        attn_out[:, cols] = mm(low.reshape(4 * WIN, WIN), vbd, TN).astype(BF16)
        qgrad = mm(dscore.reshape(4 * WIN, WIN), kbd, TN).astype(BF16)
        kgrad = mm(lanes(dscore), qbd).astype(BF16)
        vgrad = mm(lanes(low), dbd).astype(BF16)
        outs[1, :, cols] = mm(place, qgrad).astype(BF16)
        outs[2, :, cols] = mm(place, kgrad).astype(BF16)
        outs[3, :, cols] = mm(place, vgrad).astype(BF16)

    cot_basis = mm_split(basis[...], win[0], NT)
    part = mm_split(cot_basis, attn_out[...]) * GRAD_SCALE
    own = mm_exact(basis[...], error[...], NT)
    mine = one_hot((RANK, WIDTH), lambda r, c: c == r + me * RANK)
    to_tiles(left, part + mm_split(own, mine))
    for i in range(4):
        rows = slice(i * 256, i * 256 + 256)
        part = mm(attn_out[:, rows], win[0], TN) * GRAD_SCALE
        grad[i * 4 : i * 4 + 4] = part.reshape(4, 2, 32, WIDTH)
    proj[...] = mm(attn_out[...], weight_v[...]).astype(BF16)
    outs[0] = mm(place, proj[...]).astype(BF16)
    for copy in halo:
        copy.wait_send()


def combine_kernel(
    tiles, grad, outs, attn, cot, error,
    projected, qgrad, kgrad, vgrad, update, new_error, new_basis,
    scat, sums, gath, tiles_b, own_c, recv_c, send_x, recv_x, mid, recv_y, own_out, ret_prev, ret_next,
    send_sem, recv_sem, big_send, big_recv, local_sem,
):
    me = lax.axis_index("tok")
    rep = lax.axis_index("rep")
    core, y, x = lax.rem(me, 2), lax.rem(me // 2, 4), me // 8
    barrier = pltpu.get_barrier_semaphore()

    def greet_tok(k, carry):
        pl.semaphore_signal(barrier, inc=1, device_id={"tok": lax.rem(me + k, TOK)}, device_id_type=MESH)
        return carry

    def greet_rep(k, carry):
        pl.semaphore_signal(barrier, inc=1, device_id={"rep": lax.rem(rep + k, REP)}, device_id_type=MESH)
        return carry

    lax.fori_loop(1, TOK, greet_tok, 0)
    lax.fori_loop(1, REP, greet_rep, 0)
    local = [
        pltpu.make_async_copy(grad.at[:, core], own_c, local_sem.at[0]),
        pltpu.make_async_copy(outs.at[:, pl.ds(HALF, WIN)], own_out, local_sem.at[1]),
    ]
    for copy in local:
        copy.start()
    pl.semaphore_wait(barrier, TOK + REP - 2)

    def tok_send(n, phase, source, target):
        def step(k, carry):
            dev = lax.rem(me + k, TOK)
            pltpu.make_async_remote_copy(
                source(dev), target.at[k], send_sem.at[n, phase], recv_sem.at[n, phase],
                device_id={"tok": dev}, device_id_type=MESH,
            ).start()
            return carry

        lax.fori_loop(1, TOK, step, 0)

    def rep_send(n, target):
        def step(k, carry):
            pltpu.make_async_remote_copy(
                target.at[0], target.at[k], send_sem.at[n, 1], recv_sem.at[n, 1],
                device_id={"rep": lax.rem(rep + k, REP)}, device_id_type=MESH,
            ).start()
            return carry

        lax.fori_loop(1, REP, step, 0)

    def arrived(sem, ref, count):
        part = ref.at[pl.ds(1, count - 1)]
        pltpu.make_async_copy(part, part, sem).wait()

    def remote(src, dst, i, dev):
        return pltpu.make_async_remote_copy(
            src, dst, big_send.at[i], big_recv.at[i], device_id={"tok": dev}, device_id_type=MESH
        )

    def reduce_tok(n, source):
        arrived(recv_sem.at[n, 0], scat.at[n], TOK)
        total = source[me]
        for k in range(1, TOK):
            total = total + scat[n, k]
        sums[n, 0] = total
        rep_send(n, sums.at[n])

    def reduce_rep(n):
        arrived(recv_sem.at[n, 1], sums.at[n], REP)
        total = sums[n, lax.rem(rep + REP, REP)]
        for j in range(1, REP):
            total = total + sums[n, lax.rem(rep + REP - j, REP)]
        gath[n, 0] = total * (1.0 / REP)
        tok_send(n, 2, lambda dev: gath.at[n, 0], gath.at[n])

    def gathered(n):
        arrived(recv_sem.at[n, 2], gath.at[n], TOK)
        return jnp.concatenate(
            [
                jnp.concatenate([gath[n, lax.rem(me + TOK - (i * 8 + j), TOK)] for j in range(8)], 1)
                for i in range(4)
            ],
            0,
        )

    tok_send(0, 0, lambda dev: tiles.at[dev], scat.at[0])
    swap = remote(grad.at[:, 1 - core], recv_c, 0, me + 1 - 2 * core)
    swap.start()
    reduce_tok(0, tiles)

    local[0].wait()
    swap.wait_recv()
    over_x = []
    for k in range(1, 4):
        to = lax.rem(x + k, 4)
        send_x[k - 1] = (own_c[pl.ds(4 * to, 4)] + recv_c[pl.ds(4 * to, 4)]).astype(BF16)
        over_x.append(remote(send_x.at[k - 1], recv_x.at[k - 1], k, me + 8 * (to - x)))
        over_x[-1].start()

    reduce_rep(0)
    prev_dev, next_dev = lax.rem(me + TOK - 1, TOK), lax.rem(me + 1, TOK)
    back = [
        remote(outs.at[:, pl.ds(0, HALF)], ret_next, 7, prev_dev),
        remote(outs.at[:, pl.ds(HALF + WIN, HALF)], ret_prev, 8, next_dev),
    ]
    for copy in back:
        copy.start()

    left = gathered(0)
    mine = one_hot((RANK, WIDTH), lambda r, c: c == r + me * RANK)
    left_mine = mm_split(left, mine, NT)
    attn_left = mm_split(left, attn[...], NT)
    part = mm_split(attn_left, cot[...]) * GRAD_SCALE
    to_tiles(tiles_b, part + mm_exact(left_mine, error[...]))
    tok_send(1, 0, lambda dev: tiles_b.at[dev], scat.at[1])

    rows = lax.broadcasted_iota(jnp.int32, (RANK, 1), 0)
    eye = lax.broadcasted_iota(jnp.int32, (RANK, RANK), 0) == lax.broadcasted_iota(jnp.int32, (RANK, RANK), 1)
    gram = mm_exact(left, left, NT)
    inverse = jnp.where(eye, 1.0, 0.0)
    for j in range(RANK - 1):
        factor = jnp.where(rows > j, gram[:, j : j + 1], 0.0) * (1.0 / gram[j : j + 1, j : j + 1])
        gram, inverse = gram - factor * gram[j : j + 1], inverse - factor * inverse[j : j + 1]
    pivots = jnp.sum(jnp.where(eye, gram, 0.0), axis=1, keepdims=True)
    inverse = inverse * (1.0 / jnp.sqrt(pivots))
    ortho_mine = mm_exact(inverse, left_mine)

    reduce_tok(1, tiles_b)

    for copy in over_x:
        copy.wait_recv()
    mid[...] = own_c[pl.ds(4 * x, 4)] + recv_c[pl.ds(4 * x, 4)]
    for k in range(3):
        mid[...] += recv_x[k].astype(F32)
    over_y = []
    for k in range(1, 4):
        to = lax.rem(y + k, 4)
        over_y.append(remote(mid.at[to], recv_y.at[k - 1], 3 + k, me + 2 * (to - y)))
        over_y[-1].start()

    reduce_rep(1)
    for copy in over_y:
        copy.wait_recv()
    merged = mid[y] + recv_y[0] + recv_y[1] + recv_y[2] + error[...]
    new_error[...] = merged

    for copy in back:
        copy.wait_recv()
    local[1].wait()
    for i, out in enumerate((projected, qgrad, kgrad, vgrad)):
        out[0:HALF] = own_out[i, 0:HALF] + ret_prev[i]
        out[HALF:WIN] = own_out[i, HALF:WIN] + ret_next[i]

    product = gathered(1)
    basis_t = mm_exact(inverse, product)
    low_rank = mm_exact(ortho_mine, basis_t, TN)
    update[...] = low_rank
    new_error[...] = new_error[...] - low_rank
    new_basis[...] = basis_t.T

    for n in range(2):
        for phase, count in ((0, TOK), (1, REP), (2, TOK)):
            arrived(send_sem.at[n, phase], scat.at[n] if count == TOK else sums.at[n], count)
    swap.wait_send()
    for copy in over_x + over_y + back:
        copy.wait_send()


def body(
    query_rows, key_rows, value_rows, cotangent, out_weight, error_rows, window_shift, basis_seed
):
    basis = seeded_basis_t(basis_seed[0])
    error = error_rows[0]
    vmem = pl.BlockSpec(memory_space=pltpu.VMEM)
    anywhere = pl.BlockSpec(memory_space=pl.ANY)
    outs, grad, left, attn, cot = pl.pallas_call(
        attend_kernel,
        out_shape=(
            jax.ShapeDtypeStruct((4, 2 * WIN, WIDTH), BF16),
            jax.ShapeDtypeStruct((16, 2, RANK, WIDTH), F32),
            jax.ShapeDtypeStruct((TOK, 8, 128), F32),
            jax.ShapeDtypeStruct((WIN, WIDTH), BF16),
            jax.ShapeDtypeStruct((WIN, WIDTH), BF16),
        ),
        in_specs=[pl.BlockSpec(memory_space=pltpu.SMEM)] + [anywhere] * 5 + [vmem] * 2,
        out_specs=(vmem,) * 5,
        scratch_shapes=[
            pltpu.VMEM((4, 2 * WIN, WIDTH), BF16),
            pltpu.VMEM((WIDTH, WIDTH), BF16),
            pltpu.VMEM((4, WIN, WIDTH), BF16),
            pltpu.VMEM((WIN, WIDTH), BF16),
            pltpu.VMEM((WIN, WIDTH), BF16),
            pltpu.SemaphoreType.DMA((8,)),
            pltpu.SemaphoreType.DMA((8,)),
            pltpu.SemaphoreType.DMA((5,)),
        ],
        compiler_params=pltpu.CompilerParams(
            collective_id=0, has_side_effects=True, vmem_limit_bytes=48 * 2**20
        ),
        name="attend",
    )(window_shift, query_rows[0], key_rows[0], value_rows[0], cotangent[0], out_weight, basis, error)
    rows = jax.ShapeDtypeStruct((WIN, WIDTH), BF16)
    square = jax.ShapeDtypeStruct((RANK, WIDTH), F32)
    projected, qgrad, kgrad, vgrad, update, new_error, new_basis = pl.pallas_call(
        combine_kernel,
        out_shape=(rows,) * 4 + (square, square, jax.ShapeDtypeStruct((WIDTH, RANK), F32)),
        in_specs=[vmem, anywhere, anywhere, vmem, vmem, vmem],
        out_specs=(vmem,) * 7,
        scratch_shapes=[
            pltpu.VMEM((2, TOK, 8, 128), F32),
            pltpu.VMEM((2, REP, 8, 128), F32),
            pltpu.VMEM((2, TOK, 8, 128), F32),
            pltpu.VMEM((TOK, 8, 128), F32),
            pltpu.VMEM((16, RANK, WIDTH), F32),
            pltpu.VMEM((16, RANK, WIDTH), F32),
            pltpu.VMEM((3, 4, RANK, WIDTH), BF16),
            pltpu.VMEM((3, 4, RANK, WIDTH), BF16),
            pltpu.VMEM((4, RANK, WIDTH), F32),
            pltpu.VMEM((3, RANK, WIDTH), F32),
            pltpu.VMEM((4, WIN, WIDTH), BF16),
            pltpu.VMEM((4, HALF, WIDTH), BF16),
            pltpu.VMEM((4, HALF, WIDTH), BF16),
            pltpu.SemaphoreType.DMA((2, 3)),
            pltpu.SemaphoreType.DMA((2, 3)),
            pltpu.SemaphoreType.DMA((9,)),
            pltpu.SemaphoreType.DMA((9,)),
            pltpu.SemaphoreType.DMA((2,)),
        ],
        compiler_params=pltpu.CompilerParams(
            collective_id=1, has_side_effects=True, vmem_limit_bytes=48 * 2**20
        ),
        name="combine",
    )(left, grad, outs, attn, cot, error)
    return (
        projected[None],
        qgrad[None],
        kgrad[None],
        vgrad[None],
        update,
        new_error[None],
        new_basis,
    )


def solution(mesh):
    return jax.shard_map(
        body,
        mesh=mesh,
        in_specs=(
            P("rep", "tok", None),
            P("rep", "tok", None),
            P("rep", "tok", None),
            P("rep", "tok", None),
            P(),
            P("rep", "tok", None),
            P("rep"),
            P(),
        ),
        out_specs=(
            P("rep", "tok", None),
            P("rep", "tok", None),
            P("rep", "tok", None),
            P("rep", "tok", None),
            P("tok", None),
            P("rep", "tok", None),
            P(),
        ),
        check_vma=False,
    )
```

time: 663 us -> 109 us (0.16)
  waiting for transfers between devices: 546 us -> 0 us
  Pallas kernels: 0 us -> 95.3 us
  matrix products: 39.9 us -> 0 us
  starting transfers between devices: 27.9 us -> 0 us
  other arithmetic: 15.9 us -> 0.33 us
  between operations: 15.3 us -> 2.02 us
    psum x2 -> x0, waiting for transfers between devices: 524 us -> none  [the longest x1 269 us: body(): whole = lax.psum(whole, ('rep', 'tok')) / rep_count]
    pallas_call x0 -> x2, Pallas kernels: none -> 95.3 us  [the longest x1 70.9 us: body(): pl.pallas_call(combine_kernel, out_shape=(rows,) * 4 + (square, square, j...]
    dot_general x12 -> x0, matrix products: 35.5 us -> none  [the longest x1 6.98 us: body(): jnp.einsum('hqk,qhd->khd', dscore, query_heads, preferred_element_type=jn...]
    ppermute x4 -> x0, starting transfers between devices: 17.2 us -> none  [the longest x2 11.2 us: padded_2(): lax.ppermute(head, axis, [((i + 1) % count, i) for i in range(count)])]
    another operation x7 -> x0, other arithmetic: 11.9 us -> none  [the longest x3 3.6 us: body(): lower = jnp.linalg.cholesky(gram)]
    all_gather x1 -> x0, waiting for transfers between devices: 11.4 us -> none  [body(): lax.all_gather(upstream, 'tok', axis=0, tiled=True)]
    all_to_all x1 -> x0, starting transfers between devices: 10.6 us -> none  [body(): lax.all_to_all(attn_parts, 'tok', split_axis=1, concat_axis=0, tiled=True)]
    ppermute x4 -> x0, waiting for transfers between devices: 8.73 us -> none  [the longest x2 5.53 us: padded_2(): lax.ppermute(tail, axis, [(i, (i + 1) % count) for i in range(count)])]
  transfers between devices with their start and end apart: 8 -> 0, of which waited for: 7 -> 0; matrix products, arithmetic and copies ran while one was open for 9% -> 0% of each run, Pallas kernels for 0% -> 0%
where the time goes in v1:
time: 109 us
  Pallas kernels  95.3 us (87%)
  local copies, waits for them, and re-layouts  11.2 us (10%)
  between operations  2.02 us (2%)
    pallas_call x1, Pallas kernels, body(): pl.pallas_call(combine_kernel, out_shape=(rows,) * 4 + (square, square, j...  70.9 us
    pallas_call x1, Pallas kernels, body(): pl.pallas_call(attend_kernel, out_shape=(jax.ShapeDtypeStruct((4, 2 * WIN...  24.4 us
    unnamed x21, local copies, waits for them, and re-layouts  11.2 us

profile of v1, /device:TPU:1, one launch (start us, length us, event | category | flops | bytes accessed | tf_op | source)
XLA Modules:
  0.0 108.9 jit_solution(10722726038900593259)
XLA Ops:
  0.6 0.0 copy-start.2
  2.0 0.3 fusion.8.basis
  2.3 0.0 copy-start
  2.3 1.6 %copy-done = bf16[1024,1024]{1,0:T(8,128)(2,1)S(1)} copy-done((bf16[1024,1024]{1,0:T(8,128)(2,1)S(1)}, bf16[1024,1024]{1,0:T(8,128)(2,1)}, u32[]{:S(2)}) %copy-start) | copy-done | bytes 2097176
  3.9 0.0 copy-start.1
  3.9 0.9 copy-done.1
  4.8 0.0 copy-start.3
  4.8 0.9 copy-done.3
  5.8 0.0 copy-start.4
  5.8 0.9 copy-done.4
  6.7 0.0 copy-start.5
  6.7 0.9 copy-done.5
  7.7 0.0 copy-start.6
  7.7 0.9 copy-done.6
  8.6 24.4 %attend.1 = (bf16[4,256,1024]{2,1,0:T(8,128)(2,1)S(1)}, f32[16,2,32,1024]{3,2,1,0:T(8,128)}, f32[32,8,128]{2,1,0:T(8,128)S(1)}, bf16[128,1024]{1,0:T(8,128)(2,1)S(1)}, bf16[128,1024]{1,0:T(8,128)(2,1)S(1)}) custom-call(s32[1]{0:T(128)S(6)} %copy.22.shift, bf16[128,1024]{1,0:T(8,128)(2,1)S(1)} %bitcast.13, bf16[128,1024]{1,0:T(8,128)(2,1)S(1)} %bitcast.14, ...), custom_call_target="tpu_custom_call" | custom-call | tf_op jit(solution)/shard_map/attend/pallas_call | solution.py:335
  33.0 0.0 copy-done.2
  33.0 70.9 %combine.1 = (bf16[128,1024]{1,0:T(8,128)(2,1)S(1)}, bf16[128,1024]{1,0:T(8,128)(2,1)S(1)}, bf16[128,1024]{1,0:T(8,128)(2,1)S(1)}, bf16[128,1024]{1,0:T(8,128)(2...) custom-call(f32[32,8,128]{2,1,0:T(8,128)S(1)} %get-tuple-element.19.tiles, ...), custom_call_target="tpu_custom_call" | custom-call | tf_op jit(solution)/shard_map/combine/pallas_call | solution.py:363
  104.0 0.8 copy.15
  104.8 0.7 copy.24
  105.5 0.7 copy.25
  106.2 0.7 copy.26
  106.9 0.7 copy.27
  107.6 0.7 copy.28
  108.3 0.7 copy.29
  (2 shorter events, 0.0 us)
Async XLA Ops:
  0.6 32.4 %copy-start.2 = (f32[1,32,1024]{2,1,0:T(8,128)S(1)}, f32[1,32,1024]{2,1,0:T(8,128)}, u32[]{:S(2)}) copy-start(f32[1,32,1024]{2,1,0:T(8,128)} %param.13) | copy-start | bytes 393220
  2.3 1.6 %copy-start = (bf16[1024,1024]{1,0:T(8,128)(2,1)S(1)}, bf16[1024,1024]{1,0:T(8,128)(2,1)}, u32[]{:S(2)}) copy-start(bf16[1024,1024]{1,0:T(8,128)(2,1)} %weight.1) | copy-start | bytes 6291460
  3.9 0.9 copy-start.1
  4.8 0.9 copy-start.3
  5.8 0.9 copy-start.4
  6.7 0.9 copy-start.5
  7.7 0.9 copy-start.6

commit v2 on v1

v2 whole, which is shorter than its diff:
```python
import math

import jax
import jax.numpy as jnp
from jax import lax
from jax.experimental import pallas as pl
from jax.experimental.pallas import tpu as pltpu
from jax.sharding import PartitionSpec as P

H = 16
HD = 64
WIN = 128
HALF = 64
RANK = 32
WIDTH = 1024
TOK = 32
REP = 16
GROUP = 64
LONG = 8
GRAD_SCALE = 1.0 / 64.0
F32 = jnp.float32
BF16 = jnp.bfloat16
MESH = pl.DeviceIdType.MESH
HIGHEST = lax.Precision.HIGHEST
NN = (((1,), (0,)), ((), ()))
NT = (((1,), (1,)), ((), ()))
TN = (((0,), (0,)), ((), ()))


def seeded_basis_t(seed_value):
    row_index = jnp.arange(WIDTH, dtype=jnp.int32)[None, :]
    col_index = jnp.arange(RANK, dtype=jnp.int32)[:, None]
    mixed = (row_index * 7919 + col_index * 31337 + seed_value * 17 + 12345) % 65521
    mixed = (mixed * 3877 + 29) % 65521
    mixed = (mixed * 2011 + 7) % 65521
    return mixed.astype(F32) / 65521.0 - 0.5


def mm(a, b, dims=NN):
    return lax.dot_general(a, b, dims, preferred_element_type=F32)


def mm_exact(a, b, dims=NN):
    return lax.dot_general(a, b, dims, precision=HIGHEST, preferred_element_type=F32)


def mm_split(a, b, dims=NN):
    high = a.astype(BF16)
    rest = a - high.astype(F32)
    middle = rest.astype(BF16)
    low = (rest - middle.astype(F32)).astype(BF16)
    out = mm(jnp.concatenate([high, middle, low], 0), b, dims)
    return (out[2 * RANK :] + out[RANK : 2 * RANK]) + out[:RANK]


def one_hot(shape, row_to_col):
    rows = lax.broadcasted_iota(jnp.int32, shape, 0)
    cols = lax.broadcasted_iota(jnp.int32, shape, 1)
    return jnp.where(row_to_col(rows, cols), 1.0, 0.0).astype(BF16)


def halo_kernel(query, key, value, cot, cat, send_sem, recv_sem, local_sem):
    me = lax.axis_index("tok")
    next_dev, prev_dev = (me + 1) & (TOK - 1), (me + TOK - 1) & (TOK - 1)
    barrier = pltpu.get_barrier_semaphore()
    for dev in (next_dev, prev_dev):
        pl.semaphore_signal(barrier, inc=1, device_id={"tok": dev}, device_id_type=MESH)
    sources = (cot, key, query, value)
    copies = [
        pltpu.make_async_copy(src, cat.at[i, pl.ds(HALF, WIN)], local_sem.at[i])
        for i, src in enumerate(sources)
    ]
    for copy in copies:
        copy.start()
    pl.semaphore_wait(barrier, 2)
    for i, src in enumerate(sources):
        for j, (rows, place, dev) in enumerate(((0, HALF + WIN, prev_dev), (HALF, 0, next_dev))):
            copies.append(
                pltpu.make_async_remote_copy(
                    src.at[pl.ds(rows, HALF)], cat.at[i, pl.ds(place, HALF)],
                    send_sem.at[2 * i + j], recv_sem.at[2 * i + j],
                    device_id={"tok": dev}, device_id_type=MESH,
                )
            )
            copies[-1].start()
    for copy in copies:
        copy.wait()


def main_kernel(
    shift, cat, weight, basis, error_rows,
    projected, qgrad, kgrad, vgrad, update, new_error, new_basis,
    weight_v, error, win, dattn, attn, probs_s, outs, grad, recv_c, send_x, recv_x, mid, send_y, recv_y,
    ret_prev, ret_next, chunks, scat, sums, gath, whole,
    send_sem, recv_sem, big_send, big_recv, local_sem,
):
    me = lax.axis_index("tok")
    rep = lax.axis_index("rep")
    core, y_hi, x = me & 1, (me >> 1) & 3, me >> 3
    y_lo, z = rep >> 3, rep & 7
    member = (x * 2 + core) * 8 + z
    y = y_hi * 2 + y_lo
    next_dev, prev_dev = (me + 1) & (TOK - 1), (me + TOK - 1) & (TOK - 1)

    def in_group(k):
        to = (member + k) & (GROUP - 1)
        return to, {"tok": ((to >> 4) << 3) + y_hi * 2 + ((to >> 3) & 1), "rep": y_lo * 8 + (to & 7)}

    def in_y(k):
        to = (y + k) & (LONG - 1)
        return {"tok": x * 8 + (to >> 1) * 2 + core, "rep": (to & 1) * 8 + z}

    barrier = pltpu.get_barrier_semaphore()

    def greet(dev):
        pl.semaphore_signal(barrier, inc=1, device_id=dev, device_id_type=MESH)

    @pl.loop(1, GROUP)
    def _(k):
        greet(in_group(k)[1])

    @pl.loop(1, LONG)
    def _(k):
        greet(in_y(k))

    outer = core * next_dev + (1 - core) * prev_dev
    greet({"tok": outer})
    load_weight = pltpu.make_async_copy(weight, weight_v, local_sem.at[0])
    load_error = pltpu.make_async_copy(error_rows, error, local_sem.at[1])
    load_error.start()
    load_weight.start()

    def group_send(n, phase, source, target):
        @pl.loop(1, GROUP)
        def _(k):
            to, dev = in_group(k)
            pltpu.make_async_remote_copy(
                source(to), target(k), send_sem.at[n, phase], recv_sem.at[n, phase],
                device_id=dev, device_id_type=MESH,
            ).start()

    def arrived(sem, ref, count):
        part = ref.at[pl.ds(1, count - 1)]
        pltpu.make_async_copy(part, part, sem).wait()

    def remote(src, dst, i, dev):
        return pltpu.make_async_remote_copy(
            src, dst, big_send.at[i], big_recv.at[i], device_id={"tok": dev}, device_id_type=MESH
        )

    def scatter(n, field):
        for i in range(8):
            for j in range(8):
                chunks[n, i * 8 + j] = field[i * 4 : i * 4 + 4, j * 128 : j * 128 + 128]
        group_send(n, 0, lambda to: chunks.at[n, to], lambda k: scat.at[n, k])

    def reduce_group(n):
        arrived(recv_sem.at[n, 0], scat.at[n], GROUP)
        total = chunks[n, member]
        for k in range(1, GROUP):
            total = total + scat[n, k]
        sums[n, y] = total

        @pl.loop(1, LONG)
        def _(k):
            pltpu.make_async_remote_copy(
                sums.at[n, y], sums.at[n, y], send_sem.at[n, 1], recv_sem.at[n, 1],
                device_id=in_y(k), device_id_type=MESH,
            ).start()

    def reduce_y(n):
        arrived(recv_sem.at[n, 1], sums.at[n], LONG)
        total = sums[n, 0]
        for j in range(1, LONG):
            total = total + sums[n, j]
        gath[n, member] = total * (1.0 / REP)
        group_send(n, 2, lambda to: gath.at[n, member], lambda k: gath.at[n, member])

    def gathered(n):
        arrived(recv_sem.at[n, 2], gath.at[n], GROUP)
        for i in range(8):
            for j in range(8):
                whole[n, i * 4 : i * 4 + 4, j * 128 : j * 128 + 128] = gath[n, i * 8 + j]
        return whole[n]

    offset = shift[0]
    start = jnp.where(offset <= HALF, offset + HALF, offset - HALF)
    pick = one_hot((WIN, 2 * WIN), lambda r, c: c == r + start)
    place = one_hot((2 * WIN, WIN), lambda r, c: r == c + start)
    head = lax.broadcasted_iota(jnp.int32, (WIN, 4 * HD), 1) // HD
    masks = [jnp.where(head == h, 1.0, 0.0).astype(BF16) for h in range(4)]

    def spread(a):
        return jnp.concatenate([a * mask for mask in masks], 0)

    def lanes(a):
        return jnp.concatenate([a[h] for h in range(4)], 1)

    for i in range(4):
        win[i] = mm(pick, cat[i]).astype(BF16)
    for g in range(4):
        cols = slice(g * 256, g * 256 + 256)
        kbd, vbd = spread(win[1, :, cols]), spread(win[3, :, cols])
        scores = (mm(kbd, win[2, :, cols], NT) * 0.125).reshape(4, WIN, WIN)
        expo = jnp.exp(scores - jnp.max(scores, axis=1, keepdims=True))
        probs = expo / jnp.sum(expo, axis=1, keepdims=True)
        probs_s[g] = probs
        attn[:, cols] = mm(probs.astype(BF16).reshape(4 * WIN, WIN), vbd, TN).astype(BF16)

    cot = win.at[0]
    cot_basis = mm_split(basis[...], cot[...], NT)
    part = mm_split(cot_basis, attn[...]) * GRAD_SCALE
    load_error.wait()
    own = mm_exact(basis[...], error[...], NT)
    mine = one_hot((RANK, WIDTH), lambda r, c: c == r + me * RANK)
    part = part + mm_split(own, mine)
    pl.semaphore_wait(barrier, GROUP + LONG - 1)
    scatter(0, part)

    for i in range(4):
        rows = slice(i * 256, i * 256 + 256)
        part = mm(attn[:, rows], cot[...], TN) * GRAD_SCALE
        grad[i * 4 : i * 4 + 4] = part.reshape(4, 2, 32, WIDTH)
    swap = remote(grad.at[:, 1 - core], recv_c, 0, me + 1 - 2 * core)
    swap.start()

    load_weight.wait()
    dattn[...] = mm(cot[...], weight_v[...], NT).astype(BF16)

    def backward(g):
        cols = slice(g * 256, g * 256 + 256)
        k4, q4, v4, d4 = win[1, :, cols], win[2, :, cols], win[3, :, cols], dattn[:, cols]
        probs = probs_s[g]
        low = probs.astype(BF16)
        dprob = mm(spread(v4), d4, NT).reshape(4, WIN, WIN)
        delta = jnp.sum(probs * dprob, axis=1, keepdims=True)
        dscore = (probs * (dprob - delta) * 0.125).astype(BF16)
        results = (
            mm(dscore.reshape(4 * WIN, WIN), spread(k4), TN),
            mm(lanes(dscore), spread(q4)),
            mm(lanes(low), spread(d4)),
        )
        for i, result in enumerate(results):
            outs[1 + i, :, cols] = mm(place, result.astype(BF16)).astype(BF16)

    backward(0)
    backward(1)
    reduce_group(0)

    def ring(index, count_dev, send, recv, first, part, half):
        up, down, far = (index + 1) & 3, (index + 3) & 3, (index + 2) & 3
        to_up, to_down = count_dev(up), count_dev(down)
        send[0, 0] = part(far, 0).astype(BF16)
        send[1, 0] = part(far, 1).astype(BF16)
        send[0, 1] = part(up, 1).astype(BF16)
        send[1, 1] = part(down, 0).astype(BF16)
        copies = {
            (d, i): remote(send.at[d, i], recv.at[d, i], first + 3 * d + i, dev)
            for d, dev in enumerate((to_up, to_down))
            for i in range(3)
        }
        for i in range(2):
            for d in range(2):
                copies[d, i].start()

        def forward():
            for d, (to, rows) in enumerate(((up, 0), (down, 1))):
                copies[d, 0].wait_recv()
                send[d, 2] = (part(to, rows) + recv[d, 0].astype(F32)).astype(BF16)
                copies[d, 2].start()

        def total(rows):
            one, two = ((0, 2), (1, 1)) if rows == 0 else ((1, 2), (0, 1))
            return part(index, rows) + recv[one].astype(F32) + recv[two].astype(F32)

        def wait_total():
            for d in range(2):
                copies[d, 1].wait_recv()
                copies[d, 2].wait_recv()

        return copies, forward, wait_total, total

    def part_x(to, rows):
        blocks = pl.ds(4 * to + 2 * rows, 2)
        return grad[blocks, core] + recv_c[blocks]

    def part_y(to, rows):
        return mid[to, rows * 16 : rows * 16 + 16]

    swap.wait_recv()
    copies_x, forward_x, wait_x, total_x = ring(
        x, lambda to: to * 8 + y_hi * 2 + core, send_x, recv_x, 1, part_x, 2
    )

    backward(2)
    backward(3)
    outs[0] = mm(place, mm(attn[...], weight_v[...]).astype(BF16)).astype(BF16)
    reduce_y(0)
    back = [
        remote(outs.at[:, pl.ds(0, HALF)], ret_next, 13, prev_dev),
        remote(outs.at[:, pl.ds(HALF + WIN, HALF)], ret_prev, 14, next_dev),
    ]
    for copy in back:
        copy.start()
    forward_x()

    left = gathered(0)
    left_mine = mm_split(left, mine, NT)
    attn_left = mm_split(left, attn[...], NT)
    part = mm_split(attn_left, cot[...]) * GRAD_SCALE
    scatter(1, part + mm_exact(left_mine, error[...]))

    rows = lax.broadcasted_iota(jnp.int32, (RANK, 1), 0)
    eye = lax.broadcasted_iota(jnp.int32, (RANK, RANK), 0) == lax.broadcasted_iota(jnp.int32, (RANK, RANK), 1)
    gram = mm_exact(left, left, NT)
    inverse = jnp.where(eye, 1.0, 0.0)
    for j in range(RANK - 1):
        factor = jnp.where(rows > j, gram[:, j : j + 1], 0.0) * (1.0 / gram[j : j + 1, j : j + 1])
        gram, inverse = gram - factor * gram[j : j + 1], inverse - factor * inverse[j : j + 1]
    pivots = jnp.sum(jnp.where(eye, gram, 0.0), axis=1, keepdims=True)
    inverse = inverse * (1.0 / jnp.sqrt(pivots))
    ortho_mine = mm_exact(inverse, left_mine)

    reduce_group(1)
    wait_x()
    for rows in range(2):
        mid[2 * rows : 2 * rows + 2] = total_x(rows)
    copies_y, forward_y, wait_y, total_y = ring(
        y_hi, lambda to: x * 8 + to * 2 + core, send_y, recv_y, 7, part_y, 16
    )
    reduce_y(1)
    forward_y()

    for copy in back:
        copy.wait_recv()
    for i, out in enumerate((projected, qgrad, kgrad, vgrad)):
        out[0:HALF] = outs[i, HALF:WIN] + ret_prev[i]
        out[HALF:WIN] = outs[i, WIN : WIN + HALF] + ret_next[i]

    product = gathered(1)
    basis_t = mm_exact(inverse, product)
    low_rank = mm_exact(ortho_mine, basis_t, TN)
    update[...] = low_rank
    new_basis[...] = basis_t
    wait_y()
    for rows in range(2):
        at = slice(rows * 16, rows * 16 + 16)
        new_error[at] = total_y(rows) + error[at] - low_rank[at]

    for n in range(2):
        for phase, ref, count in ((0, scat, GROUP), (1, sums, LONG), (2, gath, GROUP)):
            arrived(send_sem.at[n, phase], ref.at[n], count)
    swap.wait_send()
    for copy in [*copies_x.values(), *copies_y.values(), *back]:
        copy.wait_send()


def place_kernel(*refs):
    count = len(refs) // 2
    sems = refs[-1]
    copies = [pltpu.make_async_copy(refs[i], refs[count + i], sems.at[i]) for i in range(count)]
    for copy in copies:
        copy.start()
    for copy in copies:
        copy.wait()


def stay(array):
    return pltpu.with_memory_space_constraint(array, pltpu.HBM)


def body(
    query_rows, key_rows, value_rows, cotangent, out_weight, error_rows, window_shift, basis_seed
):
    basis = seeded_basis_t(basis_seed[0])
    error = error_rows[0]
    vmem = pl.BlockSpec(memory_space=pltpu.VMEM)
    hbm = pl.BlockSpec(memory_space=pltpu.HBM)
    cat = pl.pallas_call(
        halo_kernel,
        out_shape=jax.ShapeDtypeStruct((4, 2 * WIN, WIDTH), BF16),
        in_specs=[hbm] * 4,
        out_specs=vmem,
        scratch_shapes=[
            pltpu.SemaphoreType.DMA((8,)),
            pltpu.SemaphoreType.DMA((8,)),
            pltpu.SemaphoreType.DMA((4,)),
        ],
        compiler_params=pltpu.CompilerParams(collective_id=0, has_side_effects=True, vmem_limit_bytes=8 * 2**20),
        name="halo",
    )(*(stay(rows[0]) for rows in (query_rows, key_rows, value_rows, cotangent)))
    rows = jax.ShapeDtypeStruct((WIN, WIDTH), BF16)
    square = jax.ShapeDtypeStruct((RANK, WIDTH), F32)
    results = (rows,) * 4 + (square,) * 3
    parts = pl.pallas_call(
        main_kernel,
        out_shape=results,
        in_specs=[pl.BlockSpec(memory_space=pltpu.SMEM), vmem, hbm, vmem, hbm],
        out_specs=(vmem,) * 7,
        scratch_shapes=[
            pltpu.VMEM((WIDTH, WIDTH), BF16),
            pltpu.VMEM((RANK, WIDTH), F32),
            pltpu.VMEM((4, WIN, WIDTH), BF16),
            pltpu.VMEM((WIN, WIDTH), BF16),
            pltpu.VMEM((WIN, WIDTH), BF16),
            pltpu.VMEM((4, 4, WIN, WIN), F32),
            pltpu.VMEM((4, 2 * WIN, WIDTH), BF16),
            pltpu.VMEM((16, 2, RANK, WIDTH), F32),
            pltpu.VMEM((16, RANK, WIDTH), F32),
            pltpu.VMEM((2, 3, 2, RANK, WIDTH), BF16),
            pltpu.VMEM((2, 3, 2, RANK, WIDTH), BF16),
            pltpu.VMEM((4, RANK, WIDTH), F32),
            pltpu.VMEM((2, 3, 16, WIDTH), BF16),
            pltpu.VMEM((2, 3, 16, WIDTH), BF16),
            pltpu.VMEM((4, HALF, WIDTH), BF16),
            pltpu.VMEM((4, HALF, WIDTH), BF16),
            pltpu.VMEM((2, GROUP, 4, 128), F32),
            pltpu.VMEM((2, GROUP, 4, 128), F32),
            pltpu.VMEM((2, LONG, 4, 128), F32),
            pltpu.VMEM((2, GROUP, 4, 128), F32),
            pltpu.VMEM((2, RANK, WIDTH), F32),
            pltpu.SemaphoreType.DMA((2, 3)),
            pltpu.SemaphoreType.DMA((2, 3)),
            pltpu.SemaphoreType.DMA((15,)),
            pltpu.SemaphoreType.DMA((15,)),
            pltpu.SemaphoreType.DMA((2,)),
        ],
        compiler_params=pltpu.CompilerParams(
            collective_id=1, has_side_effects=True, vmem_limit_bytes=32 * 2**20
        ),
        name="main",
    )(window_shift, cat, stay(out_weight), basis, stay(error))
    projected, qgrad, kgrad, vgrad, update, new_error, new_basis = pl.pallas_call(
        place_kernel,
        out_shape=results,
        in_specs=[vmem] * 7,
        out_specs=(hbm,) * 7,
        scratch_shapes=[pltpu.SemaphoreType.DMA((7,))],
        compiler_params=pltpu.CompilerParams(vmem_limit_bytes=8 * 2**20),
        name="place",
    )(*parts)
    return (
        projected[None],
        qgrad[None],
        kgrad[None],
        vgrad[None],
        update,
        new_error[None],
        new_basis.T,
    )


def solution(mesh):
    return jax.shard_map(
        body,
        mesh=mesh,
        in_specs=(
            P("rep", "tok", None),
            P("rep", "tok", None),
            P("rep", "tok", None),
            P("rep", "tok", None),
            P(),
            P("rep", "tok", None),
            P("rep"),
            P(),
        ),
        out_specs=(
            P("rep", "tok", None),
            P("rep", "tok", None),
            P("rep", "tok", None),
            P("rep", "tok", None),
            P("tok", None),
            P("rep", "tok", None),
            P(),
        ),
        check_vma=False,
    )
```

time: 109 us -> 77.4 us (0.71)
  Pallas kernels: 95.3 us -> 75 us
  local copies, waits for them, and re-layouts: 11.2 us -> 0 us
    pallas_call x2 -> x3, Pallas kernels: 95.3 us -> 75 us  [the longest x1 54.3 us: body(): pl.pallas_call(main_kernel, out_shape=results, in_specs=[pl.BlockSpec(mem...]
    unnamed x21 -> x0, local copies, waits for them, and re-layouts: 11.2 us -> none
where the time goes in v2:
time: 77.4 us; the launch traced here: 77.2 us
  Pallas kernels  75 us (97%)
  between operations  1.96 us (3%)
    pallas_call x1, Pallas kernels, body(): pl.pallas_call(main_kernel, out_shape=results, in_specs=[pl.BlockSpec(mem...  54.3 us
    pallas_call x1, Pallas kernels, body(): pl.pallas_call(halo_kernel, out_shape=jax.ShapeDtypeStruct((4, 2 * WIN, W...  19.5 us

profile of v2, /device:TPU:1, one launch (start us, length us, event | category | flops | bytes accessed | tf_op | source)
XLA Modules:
  0.0 77.2 jit_solution(7279606041292373761)
XLA Ops:
  1.9 0.3 fusion.8.basis
  2.3 19.5 %halo.1.cat = bf16[4,256,1024]{2,1,0:T(8,128)(2,1)S(1)} custom-call(bf16[128,1024]{1,0:T(8,128)(2,1)} %bitcast.12, bf16[128,1024]{1,0:T(8,128)(2,1)} %bitcast.13, bf16[128,1024]{1,0:T(8,128)(2,1)} %bitcast.14, bf16[128,1024]{1,0:T(8,128)(2,1)} %bitcast.15), custom_call_target="tpu_custom_call" | custom-call | tf_op jit(solution)/shard_map/halo/pallas_call | solution.py:379
  21.8 54.3 %main.1 = (bf16[128,1024]{1,0:T(8,128)(2,1)S(1)}, bf16[128,1024]{1,0:T(8,128)(2,1)S(1)}, bf16[128,1024]{1,0:T(8,128)(2,1)S(1)}, bf16[128,1024]{1,0:T(8,128)(2,1)...) custom-call(s32[1]{0:T(128)S(6)} %copy.15.shift, ...), custom_call_target="tpu_custom_call" | custom-call | tf_op jit(solution)/shard_map/main/pallas_call | solution.py:395
  76.1 1.2 %place.1 = (bf16[128,1024]{1,0:T(8,128)(2,1)}, bf16[128,1024]{1,0:T(8,128)(2,1)}, bf16[128,1024]{1,0:T(8,128)(2,1)}, bf16[128,1024]{1,0:T(8,128)(2,1)}, f32[32,1...) custom-call(bf16[128,1024]{1,0:T(8,128)(2,1)S(1)} %get-tuple-element.21.refs_0_, ...), custom_call_target="tpu_custom_call" | custom-call | tf_op jit(solution)/shard_map/place/pallas_call | solution.py:433
  (2 shorter events, 0.0 us)

commit v3 on v2

v3 whole, which is shorter than its diff:
```python
import math

import jax
import jax.numpy as jnp
from jax import lax
from jax.experimental import pallas as pl
from jax.experimental.pallas import tpu as pltpu
from jax.sharding import PartitionSpec as P

H = 16
HD = 64
WIN = 128
HALF = 64
RANK = 32
WIDTH = 1024
TOK = 32
REP = 16
LINE = 8
PRIME = 65521
GRAD_SCALE = 1.0 / 64.0
F32 = jnp.float32
BF16 = jnp.bfloat16
MESH = pl.DeviceIdType.MESH
HIGHEST = lax.Precision.HIGHEST
NN = (((1,), (0,)), ((), ()))
NT = (((1,), (1,)), ((), ()))
TN = (((0,), (0,)), ((), ()))


def mod_prime(a):
    rest = a - (a.astype(F32) * (1.0 / PRIME)).astype(jnp.int32) * PRIME
    rest = jnp.where(rest < 0, rest + PRIME, rest)
    return jnp.where(rest >= PRIME, rest - PRIME, rest)


def seeded_basis_t(seed_value):
    row_index = lax.broadcasted_iota(jnp.int32, (RANK, WIDTH), 1)
    col_index = lax.broadcasted_iota(jnp.int32, (RANK, WIDTH), 0)
    mixed = mod_prime(row_index * 7919 + col_index * 31337 + (seed_value * 17 + 12345))
    mixed = mod_prime(mixed * 3877 + 29)
    mixed = mod_prime(mixed * 2011 + 7)
    return mixed.astype(F32) / 65521.0 - 0.5


def mm(a, b, dims=NN):
    return lax.dot_general(a, b, dims, preferred_element_type=F32)


def mm_exact(a, b, dims=NN):
    return lax.dot_general(a, b, dims, precision=HIGHEST, preferred_element_type=F32)


def mm_split(a, b, dims=NN):
    high = a.astype(BF16)
    rest = a - high.astype(F32)
    middle = rest.astype(BF16)
    low = (rest - middle.astype(F32)).astype(BF16)
    out = mm(jnp.concatenate([high, middle, low], 0), b, dims)
    return (out[2 * RANK :] + out[RANK : 2 * RANK]) + out[:RANK]


def one_hot(shape, row_to_col):
    rows = lax.broadcasted_iota(jnp.int32, shape, 0)
    cols = lax.broadcasted_iota(jnp.int32, shape, 1)
    return jnp.where(row_to_col(rows, cols), 1.0, 0.0).astype(BF16)


def halo_kernel(
    seed, query, key, value, cot, error,
    cat, cot_basis, basis, error_left,
    cot_v, error_v, send_sem, recv_sem, local_sem,
):
    me = lax.axis_index("tok")
    next_dev, prev_dev = (me + 1) & (TOK - 1), (me + TOK - 1) & (TOK - 1)
    barrier = pltpu.get_barrier_semaphore()
    for dev in (next_dev, prev_dev):
        pl.semaphore_signal(barrier, inc=1, device_id={"tok": dev}, device_id_type=MESH)
    load_cot = pltpu.make_async_copy(cot, cot_v, local_sem.at[3])
    load_error = pltpu.make_async_copy(error, error_v, local_sem.at[4])
    load_cot.start()
    load_error.start()
    sources = (key, query, value)
    copies = [
        pltpu.make_async_copy(src, cat.at[i, pl.ds(HALF, WIN)], local_sem.at[i])
        for i, src in enumerate(sources)
    ]
    for copy in copies:
        copy.start()
    pl.semaphore_wait(barrier, 2)

    def remote(src, dst, i, dev):
        copies.append(
            pltpu.make_async_remote_copy(
                src, dst, send_sem.at[i], recv_sem.at[i], device_id={"tok": dev}, device_id_type=MESH
            )
        )
        copies[-1].start()

    for i, src in enumerate(sources):
        remote(src.at[pl.ds(0, HALF)], cat.at[i, pl.ds(HALF + WIN, HALF)], 2 * i, prev_dev)
        remote(src.at[pl.ds(HALF, HALF)], cat.at[i, pl.ds(0, HALF)], 2 * i + 1, next_dev)

    basis[...] = seeded_basis_t(seed[0])
    load_cot.wait()
    cot_basis[1] = mm_split(basis[...], cot_v[...], NT)
    remote(cot_basis.at[1], cot_basis.at[2], 6, prev_dev)
    remote(cot_basis.at[1], cot_basis.at[0], 7, next_dev)
    load_error.wait()
    own = mm_exact(basis[...], error_v[...], NT)
    mine = one_hot((RANK, WIDTH), lambda r, c: c == r + me * RANK)
    error_left[...] = mm_split(own, mine)
    for copy in copies:
        copy.wait()


def main_kernel(
    shift, cat, cot_basis, basis, error_left, weight, cot_rows, error_rows,
    projected, qgrad, kgrad, vgrad, update, new_error, new_basis,
    weight_v, error, cot_cat, win, dattn, attn, probs_s, outs, grad, grad_low, recv_c, send_x, recv_x, mid, send_y, recv_y,
    ret_prev, ret_next, chunks, scat, sums, gath,
    send_sem, recv_sem, big_send, big_recv, local_sem,
):
    me = lax.axis_index("tok")
    rep = lax.axis_index("rep")
    core, y_hi, x = me & 1, (me >> 1) & 3, me >> 3
    y_lo, z = rep >> 3, rep & 7
    pair = x * 2 + core
    y = y_hi * 2 + y_lo
    next_dev, prev_dev = (me + 1) & (TOK - 1), (me + TOK - 1) & (TOK - 1)

    def others(index):
        return [(index + k) & (LINE - 1) for k in (4, 3, 5, 2, 6, 1, 7)]

    steps = ((2, 0), (2, 1), (1, 0), (3, 0), (1, 1), (3, 1), (0, 1))
    along_x = [{"tok": ((x + i) & 3) * 8 + y_hi * 2 + (core ^ j)} for i, j in steps]
    along_y = [{"tok": x * 8 + (to >> 1) * 2 + core, "rep": (to & 1) * 8 + z} for to in others(y)]
    along_z = [(to, {"rep": y_lo * 8 + to}) for to in others(z)]
    barrier = pltpu.get_barrier_semaphore()

    def greet(dev):
        pl.semaphore_signal(barrier, inc=1, device_id=dev, device_id_type=MESH)

    for dev in [dev for _, dev in along_z] + along_y + along_x:
        greet(dev)
    outer = core * next_dev + (1 - core) * prev_dev
    greet({"tok": outer})
    load_weight = pltpu.make_async_copy(weight, weight_v, local_sem.at[0])
    load_error = pltpu.make_async_copy(error_rows, error, local_sem.at[1])
    load_cot = pltpu.make_async_copy(cot_rows, cot_cat.at[pl.ds(HALF, WIN)], local_sem.at[2])
    load_weight.start()
    load_cot.start()
    load_error.start()

    def small(src, dst, sems, dev):
        send, recv = send_sem.at[sems], recv_sem.at[sems]
        pltpu.make_async_remote_copy(src, dst, send, recv, device_id=dev, device_id_type=MESH).start()

    def arrived(sem, ref):
        part = ref.at[pl.ds(1, LINE - 1)]
        pltpu.make_async_copy(part, part, sem).wait()

    def remote(src, dst, i, dev):
        return pltpu.make_async_remote_copy(
            src, dst, big_send.at[i], big_recv.at[i], device_id={"tok": dev}, device_id_type=MESH
        )

    def scatter(n, field):
        for i in range(LINE):
            chunks[n, i] = field[:, i * 128 : i * 128 + 128]
        for k, (to, dev) in enumerate(along_z):
            small(chunks.at[n, to], scat.at[n, 1 + k], 4 * n, dev)

    def line_send(n, line, total):
        index, devs = ((pair, along_x), (y, along_y))[line]
        sums[n, line, index] = total
        for dev in devs:
            small(sums.at[n, line, index], sums.at[n, line, index], 4 * n + 1 + line, dev)

    def line_sum(n, line):
        arrived(recv_sem.at[4 * n + 1 + line], sums.at[n, line])
        total = sums[n, line, 0]
        for j in range(1, LINE):
            total = total + sums[n, line, j]
        return total

    def sum_group(n):
        arrived(recv_sem.at[4 * n], scat.at[n])
        total = chunks[n, z]
        for k in range(1, LINE):
            total = total + scat[n, k]
        line_send(n, 0, total)

    def sum_first(n):
        line_send(n, 1, line_sum(n, 0))

    def sum_second(n):
        gath[n, z] = line_sum(n, 1) * (1.0 / REP)
        for _, dev in along_z:
            small(gath.at[n, z], gath.at[n, z], 4 * n + 3, dev)

    def gathered(n):
        arrived(recv_sem.at[4 * n + 3], gath.at[n])
        return jnp.concatenate([gath[n, i] for i in range(LINE)], 1)

    def sent(n):
        for i, ref in enumerate((scat.at[n], sums.at[n, 0], sums.at[n, 1], gath.at[n])):
            arrived(send_sem.at[4 * n + i], ref)

    offset = shift[0]
    start = jnp.where(offset <= HALF, offset + HALF, offset - HALF)
    pick = one_hot((WIN, 2 * WIN), lambda r, c: c == r + start)
    place = one_hot((2 * WIN, WIN), lambda r, c: r == c + start)
    head = lax.broadcasted_iota(jnp.int32, (WIN, 4 * HD), 1) // HD
    masks = [jnp.where(head == h, 1.0, 0.0).astype(BF16) for h in range(4)]

    def spread(a):
        return jnp.concatenate([a * mask for mask in masks], 0)

    def lanes(a):
        return jnp.concatenate([a[h] for h in range(4)], 1)

    for i in range(3):
        win[1 + i] = mm(pick, cat[i]).astype(BF16)
    for g in range(4):
        cols = slice(g * 256, g * 256 + 256)
        kbd, vbd = spread(win[1, :, cols]), spread(win[3, :, cols])
        scores = (mm(kbd, win[2, :, cols], NT) * 0.125).reshape(4, WIN, WIN)
        expo = jnp.exp(scores - jnp.max(scores, axis=1, keepdims=True))
        probs = expo / jnp.sum(expo, axis=1, keepdims=True)
        probs_s[g] = probs
        attn[:, cols] = mm(probs.astype(BF16).reshape(4 * WIN, WIN), vbd, TN).astype(BF16)

    cot_cols = jnp.concatenate([cot_basis[i] for i in range(3)], 1)
    pick_cols = one_hot((3 * WIN, WIN), lambda r, c: r == c + start + HALF)
    part = mm_split(mm_split(cot_cols, pick_cols), attn[...]) * GRAD_SCALE + error_left[...]
    pl.semaphore_wait(barrier, 3 * (LINE - 1) + 1)
    scatter(0, part)
    cot_halo = [
        remote(cot_rows.at[pl.ds(0, HALF)], cot_cat.at[pl.ds(HALF + WIN, HALF)], 20, prev_dev),
        remote(cot_rows.at[pl.ds(HALF, HALF)], cot_cat.at[pl.ds(0, HALF)], 21, next_dev),
    ]
    for copy in cot_halo:
        copy.start()

    def send_back(i, arrays, cols):
        copies = [
            remote(outs.at[arrays, pl.ds(0, HALF), cols], ret_next.at[arrays, :, cols], i, prev_dev),
            remote(outs.at[arrays, pl.ds(HALF + WIN, HALF), cols], ret_prev.at[arrays, :, cols], i + 1, next_dev),
        ]
        for copy in copies:
            copy.start()
        return copies

    load_weight.wait()
    outs[0] = mm(place, mm(attn[...], weight_v[...]).astype(BF16)).astype(BF16)
    load_cot.wait()
    sum_group(0)
    for copy in cot_halo:
        copy.wait_recv()
    back = send_back(13, pl.ds(0, 1), pl.ds(0, WIDTH))
    cot = win.at[0]
    cot[...] = mm(pick, cot_cat[...]).astype(BF16)

    swaps = []
    for i, step in enumerate((2, 1, 3, 0)):
        to = (x + step) & 3
        cols = pl.ds(pl.multiple_of(to * 256, 256), 256)
        part = (mm(attn[:, cols], cot[...], TN) * GRAD_SCALE).reshape(4, 2, 32, WIDTH)
        blocks = pl.ds(4 * to, 4)
        grad[blocks] = jnp.where(core == 0, part[:, 0], part[:, 1])
        grad_low[blocks] = jnp.where(core == 0, part[:, 1], part[:, 0]).astype(BF16)
        swaps.append(remote(grad_low.at[blocks], recv_c.at[blocks], (0, 15, 16, 17)[i], me + 1 - 2 * core))
        swaps[-1].start()

    dattn[...] = mm(cot[...], weight_v[...], NT).astype(BF16)

    def backward(g):
        cols = slice(g * 256, g * 256 + 256)
        k4, q4, v4, d4 = win[1, :, cols], win[2, :, cols], win[3, :, cols], dattn[:, cols]
        probs = probs_s[g]
        low = probs.astype(BF16)
        dprob = mm(spread(v4), d4, NT).reshape(4, WIN, WIN)
        delta = jnp.sum(probs * dprob, axis=1, keepdims=True)
        dscore = (probs * (dprob - delta) * 0.125).astype(BF16)
        results = (
            mm(dscore.reshape(4 * WIN, WIN), spread(k4), TN),
            mm(lanes(dscore), spread(q4)),
            mm(lanes(low), spread(d4)),
        )
        for i, result in enumerate(results):
            outs[1 + i, :, cols] = mm(place, result.astype(BF16)).astype(BF16)

    def ring(index, count_dev, send, recv, first, part, ready):
        up, down, far = (index + 1) & 3, (index + 3) & 3, (index + 2) & 3
        to_up, to_down = count_dev(up), count_dev(down)
        copies = {
            (d, i): remote(send.at[d, i], recv.at[d, i], first + 3 * d + i, dev)
            for d, dev in enumerate((to_up, to_down))
            for i in range(3)
        }
        ready(0)
        for d in range(2):
            send[d, 0] = part(far, d).astype(BF16)
            copies[d, 0].start()

        def pure():
            for d, to in enumerate((up, down)):
                ready(1 + d)
                send[d, 1] = part(to, 1 - d).astype(BF16)
                copies[d, 1].start()

        def forward():
            for d, (to, rows) in enumerate(((up, 0), (down, 1))):
                copies[d, 0].wait_recv()
                send[d, 2] = (part(to, rows) + recv[d, 0].astype(F32)).astype(BF16)
                copies[d, 2].start()

        def total(rows):
            one, two = ((0, 2), (1, 1)) if rows == 0 else ((1, 2), (0, 1))
            return part(index, rows) + recv[one].astype(F32) + recv[two].astype(F32)

        def wait_total():
            ready(3)
            for d in range(2):
                copies[d, 1].wait_recv()
                copies[d, 2].wait_recv()

        return copies, pure, forward, wait_total, total

    def part_x(to, rows):
        blocks = pl.ds(4 * to + 2 * rows, 2)
        return grad[blocks] + recv_c[blocks].astype(F32)

    def part_y(to, rows):
        return mid[to, rows * 16 : rows * 16 + 16]

    backward(0)
    sum_first(0)
    copies_x, pure_x, forward_x, wait_x, total_x = ring(
        x, lambda to: to * 8 + y_hi * 2 + core, send_x, recv_x, 1, part_x, lambda i: swaps[i].wait_recv()
    )
    pure_x()
    backward(1)
    backward(2)
    backward(3)
    sum_second(0)
    back += send_back(18, pl.ds(1, 3), pl.ds(0, WIDTH))
    forward_x()

    load_error.wait()
    left = gathered(0)
    mine = one_hot((RANK, WIDTH), lambda r, c: c == r + me * RANK)
    left_mine = mm_split(left, mine, NT)
    attn_left = mm_split(left, attn[...], NT)
    part = mm_split(attn_left, cot[...]) * GRAD_SCALE
    scatter(1, part + mm_exact(left_mine, error[...]))

    wait_x()
    for rows in range(2):
        mid[2 * rows : 2 * rows + 2] = total_x(rows)
    copies_y, pure_y, forward_y, wait_y, total_y = ring(
        y_hi, lambda to: x * 8 + to * 2 + core, send_y, recv_y, 7, part_y, lambda i: None
    )
    pure_y()

    rows = lax.broadcasted_iota(jnp.int32, (RANK, 1), 0)
    eye = lax.broadcasted_iota(jnp.int32, (RANK, RANK), 0) == lax.broadcasted_iota(jnp.int32, (RANK, RANK), 1)
    gram = mm_exact(left, left, NT)
    inverse = jnp.where(eye, 1.0, 0.0)
    for j in range(RANK - 1):
        factor = jnp.where(rows > j, gram[:, j : j + 1], 0.0) * (1.0 / gram[j : j + 1, j : j + 1])
        gram, inverse = gram - factor * gram[j : j + 1], inverse - factor * inverse[j : j + 1]
    pivots = jnp.sum(jnp.where(eye, gram, 0.0), axis=1, keepdims=True)
    inverse = inverse * (1.0 / jnp.sqrt(pivots))
    ortho_mine = mm_exact(inverse, left_mine)

    sum_group(1)
    forward_y()
    sum_first(1)
    sum_second(1)

    for copy in back:
        copy.wait_recv()
    for i, out in enumerate((projected, qgrad, kgrad, vgrad)):
        out[0:HALF] = outs[i, HALF:WIN] + ret_prev[i]
        out[HALF:WIN] = outs[i, WIN : WIN + HALF] + ret_next[i]

    product = gathered(1)
    basis_t = mm_exact(inverse, product)
    low_rank = mm_exact(ortho_mine, basis_t, TN)
    update[...] = low_rank
    new_basis[...] = basis_t
    wait_y()
    for rows in range(2):
        at = slice(rows * 16, rows * 16 + 16)
        new_error[at] = total_y(rows) + error[at] - low_rank[at]

    for n in range(2):
        sent(n)
    for copy in [*swaps, *copies_x.values(), *copies_y.values(), *back, *cot_halo]:
        copy.wait_send()


def place_kernel(*refs):
    count = len(refs) // 2
    sems = refs[-1]
    copies = [pltpu.make_async_copy(refs[i], refs[count + i], sems.at[i]) for i in range(count)]
    for copy in copies:
        copy.start()
    for copy in copies:
        copy.wait()


def stay(array):
    return pltpu.with_memory_space_constraint(array, pltpu.HBM)


def body(
    query_rows, key_rows, value_rows, cotangent, out_weight, error_rows, window_shift, basis_seed
):
    error = stay(error_rows[0])
    cot_rows = stay(cotangent[0])
    smem = pl.BlockSpec(memory_space=pltpu.SMEM)
    vmem = pl.BlockSpec(memory_space=pltpu.VMEM)
    hbm = pl.BlockSpec(memory_space=pltpu.HBM)
    square = jax.ShapeDtypeStruct((RANK, WIDTH), F32)
    cat, cot_basis, basis, error_left = pl.pallas_call(
        halo_kernel,
        out_shape=(
            jax.ShapeDtypeStruct((3, 2 * WIN, WIDTH), BF16),
            jax.ShapeDtypeStruct((3, RANK, WIN), F32),
            square,
            square,
        ),
        in_specs=[smem] + [hbm] * 5,
        out_specs=(vmem,) * 4,
        scratch_shapes=[
            pltpu.VMEM((WIN, WIDTH), BF16),
            pltpu.VMEM((RANK, WIDTH), F32),
            pltpu.SemaphoreType.DMA((8,)),
            pltpu.SemaphoreType.DMA((8,)),
            pltpu.SemaphoreType.DMA((5,)),
        ],
        compiler_params=pltpu.CompilerParams(collective_id=0, has_side_effects=True, vmem_limit_bytes=8 * 2**20),
        name="halo",
    )(basis_seed, *(stay(rows[0]) for rows in (query_rows, key_rows, value_rows)), cot_rows, error)
    rows = jax.ShapeDtypeStruct((WIN, WIDTH), BF16)
    results = (rows,) * 4 + (square,) * 3
    parts = pl.pallas_call(
        main_kernel,
        out_shape=results,
        in_specs=[smem] + [vmem] * 4 + [hbm] * 3,
        out_specs=(vmem,) * 7,
        scratch_shapes=[
            pltpu.VMEM((WIDTH, WIDTH), BF16),
            pltpu.VMEM((RANK, WIDTH), F32),
            pltpu.VMEM((2 * WIN, WIDTH), BF16),
            pltpu.VMEM((4, WIN, WIDTH), BF16),
            pltpu.VMEM((WIN, WIDTH), BF16),
            pltpu.VMEM((WIN, WIDTH), BF16),
            pltpu.VMEM((4, 4, WIN, WIN), F32),
            pltpu.VMEM((4, 2 * WIN, WIDTH), BF16),
            pltpu.VMEM((16, RANK, WIDTH), F32),
            pltpu.VMEM((16, RANK, WIDTH), BF16),
            pltpu.VMEM((16, RANK, WIDTH), BF16),
            pltpu.VMEM((2, 3, 2, RANK, WIDTH), BF16),
            pltpu.VMEM((2, 3, 2, RANK, WIDTH), BF16),
            pltpu.VMEM((4, RANK, WIDTH), F32),
            pltpu.VMEM((2, 3, 16, WIDTH), BF16),
            pltpu.VMEM((2, 3, 16, WIDTH), BF16),
            pltpu.VMEM((4, HALF, WIDTH), BF16),
            pltpu.VMEM((4, HALF, WIDTH), BF16),
            pltpu.VMEM((2, LINE, RANK, 128), F32),
            pltpu.VMEM((2, LINE, RANK, 128), F32),
            pltpu.VMEM((2, 2, LINE, RANK, 128), F32),
            pltpu.VMEM((2, LINE, RANK, 128), F32),
            pltpu.SemaphoreType.DMA((8,)),
            pltpu.SemaphoreType.DMA((8,)),
            pltpu.SemaphoreType.DMA((22,)),
            pltpu.SemaphoreType.DMA((22,)),
            pltpu.SemaphoreType.DMA((3,)),
        ],
        compiler_params=pltpu.CompilerParams(
            collective_id=1, has_side_effects=True, vmem_limit_bytes=32 * 2**20
        ),
        name="main",
    )(window_shift, cat, cot_basis, basis, error_left, stay(out_weight), cot_rows, error)
    projected, qgrad, kgrad, vgrad, update, new_error, new_basis = pl.pallas_call(
        place_kernel,
        out_shape=results,
        in_specs=[vmem] * 7,
        out_specs=(hbm,) * 7,
        scratch_shapes=[pltpu.SemaphoreType.DMA((7,))],
        compiler_params=pltpu.CompilerParams(vmem_limit_bytes=8 * 2**20),
        name="place",
    )(*parts)
    return (
        projected[None],
        qgrad[None],
        kgrad[None],
        vgrad[None],
        update,
        new_error[None],
        new_basis.T,
    )


def solution(mesh):
    return jax.shard_map(
        body,
        mesh=mesh,
        in_specs=(
            P("rep", "tok", None),
            P("rep", "tok", None),
            P("rep", "tok", None),
            P("rep", "tok", None),
            P(),
            P("rep", "tok", None),
            P("rep"),
            P(),
        ),
        out_specs=(
            P("rep", "tok", None),
            P("rep", "tok", None),
            P("rep", "tok", None),
            P("rep", "tok", None),
            P("tok", None),
            P("rep", "tok", None),
            P(),
        ),
        check_vma=False,
    )
```

time: 77.4 us -> 75.7 us (0.978); the launches traced: 77.2 us -> 74.3 us
  Pallas kernels: 75 us -> 72.4 us
    pallas_call x2, Pallas kernels: 73.8 us -> 71.2 us  [the longest x1 54.3 us: body(): pl.pallas_call(main_kernel, out_shape=results, in_specs=[smem] + [vmem] *...]
where the time goes in v3:
time: 75.7 us; the launch traced here: 74.3 us
  Pallas kernels  72.4 us (96%)
  between operations  1.94 us (3%)
    pallas_call x1, Pallas kernels, body(): pl.pallas_call(main_kernel, out_shape=results, in_specs=[smem] + [vmem] *...  54.3 us
    pallas_call x1, Pallas kernels, body(): pl.pallas_call(halo_kernel, out_shape=(jax.ShapeDtypeStruct((3, 2 * WIN,...  16.9 us

profile of v3, /device:TPU:1, one launch (start us, length us, event | category | flops | bytes accessed | tf_op | source)
XLA Modules:
  0.0 74.3 jit_solution(10152448870593278627)
XLA Ops:
  1.9 16.9 %halo.1 = (bf16[3,256,1024]{2,1,0:T(8,128)(2,1)S(1)}, f32[3,32,128]{2,1,0:T(8,128)S(1)}, f32[32,1024]{1,0:T(8,128)S(1)}, f32[32,1024]{1,0:T(8,128)S(1)}) custom-call(s32[1]{0:T(128)S(6)} %copy.16.seed, bf16[128,1024]{1,0:T(8,128)(2,1)} %bitcast.15, bf16[128,1024]{1,0:T(8,128)(2,1)} %bitcast.16, bf16[128,1024]{1,0:T(8,128)(2,1)} %bitcast.17, ...), custom_call_target="tpu_custom_call" | custom-call | tf_op jit(solution)/shard_map/halo/pallas_call | solution.py:427
  18.9 54.3 %main.1 = (bf16[128,1024]{1,0:T(8,128)(2,1)S(1)}, bf16[128,1024]{1,0:T(8,128)(2,1)S(1)}, bf16[128,1024]{1,0:T(8,128)(2,1)S(1)}, bf16[128,1024]{1,0:T(8,128)(2,1)...) custom-call(s32[1]{0:T(128)S(6)} %copy.15.shift, ...), custom_call_target="tpu_custom_call" | custom-call | tf_op jit(solution)/shard_map/main/pallas_call | solution.py:449
  73.2 1.2 %place.1 = (bf16[128,1024]{1,0:T(8,128)(2,1)}, bf16[128,1024]{1,0:T(8,128)(2,1)}, bf16[128,1024]{1,0:T(8,128)(2,1)}, bf16[128,1024]{1,0:T(8,128)(2,1)}, f32[32,1...) custom-call(bf16[128,1024]{1,0:T(8,128)(2,1)S(1)} %get-tuple-element.29.refs_0_, ...), custom_call_target="tpu_custom_call" | custom-call | tf_op jit(solution)/shard_map/place/pallas_call | solution.py:488

commit v4 on v3

--- a/solution.py
+++ b/solution.py
@@ -65,60 +65,12 @@
     return jnp.where(row_to_col(rows, cols), 1.0, 0.0).astype(BF16)
 
 
-def halo_kernel(
-    seed, query, key, value, cot, error,
-    cat, cot_basis, basis, error_left,
-    cot_v, error_v, send_sem, recv_sem, local_sem,
-):
-    me = lax.axis_index("tok")
-    next_dev, prev_dev = (me + 1) & (TOK - 1), (me + TOK - 1) & (TOK - 1)
-    barrier = pltpu.get_barrier_semaphore()
-    for dev in (next_dev, prev_dev):
-        pl.semaphore_signal(barrier, inc=1, device_id={"tok": dev}, device_id_type=MESH)
-    load_cot = pltpu.make_async_copy(cot, cot_v, local_sem.at[3])
-    load_error = pltpu.make_async_copy(error, error_v, local_sem.at[4])
-    load_cot.start()
-    load_error.start()
-    sources = (key, query, value)
-    copies = [
-        pltpu.make_async_copy(src, cat.at[i, pl.ds(HALF, WIN)], local_sem.at[i])
-        for i, src in enumerate(sources)
-    ]
-    for copy in copies:
-        copy.start()
-    pl.semaphore_wait(barrier, 2)
-
-    def remote(src, dst, i, dev):
-        copies.append(
-            pltpu.make_async_remote_copy(
-                src, dst, send_sem.at[i], recv_sem.at[i], device_id={"tok": dev}, device_id_type=MESH
-            )
-        )
-        copies[-1].start()
-
-    for i, src in enumerate(sources):
-        remote(src.at[pl.ds(0, HALF)], cat.at[i, pl.ds(HALF + WIN, HALF)], 2 * i, prev_dev)
-        remote(src.at[pl.ds(HALF, HALF)], cat.at[i, pl.ds(0, HALF)], 2 * i + 1, next_dev)
-
-    basis[...] = seeded_basis_t(seed[0])
-    load_cot.wait()
-    cot_basis[1] = mm_split(basis[...], cot_v[...], NT)
-    remote(cot_basis.at[1], cot_basis.at[2], 6, prev_dev)
-    remote(cot_basis.at[1], cot_basis.at[0], 7, next_dev)
-    load_error.wait()
-    own = mm_exact(basis[...], error_v[...], NT)
-    mine = one_hot((RANK, WIDTH), lambda r, c: c == r + me * RANK)
-    error_left[...] = mm_split(own, mine)
-    for copy in copies:
-        copy.wait()
-
-
 def main_kernel(
-    shift, cat, cot_basis, basis, error_left, weight, cot_rows, error_rows,
+    seed, shift, query, key, value, cot_rows, weight, error_rows,
     projected, qgrad, kgrad, vgrad, update, new_error, new_basis,
-    weight_v, error, cot_cat, win, dattn, attn, probs_s, outs, grad, grad_low, recv_c, send_x, recv_x, mid, send_y, recv_y,
+    cat, cot_basis, basis, error_left, weight_v, error, cot_cat, win, dattn, attn, probs_s, outs, grad, grad_low, recv_c, send_x, recv_x, mid, send_y, recv_y,
     ret_prev, ret_next, chunks, scat, sums, gath,
-    send_sem, recv_sem, big_send, big_recv, local_sem,
+    send_sem, recv_sem, big_send, big_recv, halo_send, halo_recv, local_sem,
 ):
     me = lax.axis_index("tok")
     rep = lax.axis_index("rep")
@@ -144,12 +96,44 @@
         greet(dev)
     outer = core * next_dev + (1 - core) * prev_dev
     greet({"tok": outer})
-    load_weight = pltpu.make_async_copy(weight, weight_v, local_sem.at[0])
-    load_error = pltpu.make_async_copy(error_rows, error, local_sem.at[1])
-    load_cot = pltpu.make_async_copy(cot_rows, cot_cat.at[pl.ds(HALF, WIN)], local_sem.at[2])
-    load_weight.start()
-    load_cot.start()
-    load_error.start()
+    sources = (key, query, value)
+    load_rows = [
+        pltpu.make_async_copy(src, cat.at[i, pl.ds(HALF, WIN)], local_sem.at[i]) for i, src in enumerate(sources)
+    ]
+    load_weight = pltpu.make_async_copy(weight, weight_v, local_sem.at[3])
+    load_error = pltpu.make_async_copy(error_rows, error, local_sem.at[4])
+    load_cot = pltpu.make_async_copy(cot_rows, cot_cat.at[pl.ds(HALF, WIN)], local_sem.at[5])
+    for copy in [load_cot, load_error, *load_rows, load_weight]:
+        copy.start()
+    pl.semaphore_wait(barrier, 3 * (LINE - 1) + 1)
+
+    def to_neighbours(i, first, second):
+        copies = [
+            pltpu.make_async_remote_copy(
+                src, dst, halo_send.at[2 * i + j], halo_recv.at[2 * i + j], device_id={"tok": dev}, device_id_type=MESH
+            )
+            for j, (dev, (src, dst)) in enumerate(((prev_dev, first), (next_dev, second)))
+        ]
+        for copy in copies:
+            copy.start()
+        return copies
+
+    def rows_to_neighbours(i, src, dst):
+        return to_neighbours(
+            i,
+            (src.at[pl.ds(0, HALF)], dst.at[pl.ds(HALF + WIN, HALF)]),
+            (src.at[pl.ds(HALF, HALF)], dst.at[pl.ds(0, HALF)]),
+        )
+
+    halo = [rows_to_neighbours(i, src, cat.at[i]) for i, src in enumerate(sources)]
+
+    basis[...] = seeded_basis_t(seed[0])
+    load_cot.wait()
+    cot_basis[1] = mm_split(basis[...], cot_cat[HALF : HALF + WIN], NT)
+    halo.append(to_neighbours(3, (cot_basis.at[1], cot_basis.at[2]), (cot_basis.at[1], cot_basis.at[0])))
+    load_error.wait()
+    mine = one_hot((RANK, WIDTH), lambda r, c: c == r + me * RANK)
+    error_left[...] = mm_split(mm_exact(basis[...], error[...], NT), mine)
 
     def small(src, dst, sems, dev):
         send, recv = send_sem.at[sems], recv_sem.at[sems]
@@ -219,28 +203,32 @@
     def lanes(a):
         return jnp.concatenate([a[h] for h in range(4)], 1)
 
-    for i in range(3):
+    def picked(i):
+        load_rows[i].wait()
+        for copy in halo[i]:
+            copy.wait_recv()
         win[1 + i] = mm(pick, cat[i]).astype(BF16)
+
+    picked(0)
+    picked(1)
+    cot_halo = rows_to_neighbours(4, cot_rows, cot_cat)
     for g in range(4):
         cols = slice(g * 256, g * 256 + 256)
-        kbd, vbd = spread(win[1, :, cols]), spread(win[3, :, cols])
-        scores = (mm(kbd, win[2, :, cols], NT) * 0.125).reshape(4, WIN, WIN)
+        scores = (mm(spread(win[1, :, cols]), win[2, :, cols], NT) * 0.125).reshape(4, WIN, WIN)
         expo = jnp.exp(scores - jnp.max(scores, axis=1, keepdims=True))
-        probs = expo / jnp.sum(expo, axis=1, keepdims=True)
-        probs_s[g] = probs
-        attn[:, cols] = mm(probs.astype(BF16).reshape(4 * WIN, WIN), vbd, TN).astype(BF16)
-
+        probs_s[g] = expo / jnp.sum(expo, axis=1, keepdims=True)
+    picked(2)
+    for g in range(4):
+        cols = slice(g * 256, g * 256 + 256)
+        low = probs_s[g].astype(BF16).reshape(4 * WIN, WIN)
+        attn[:, cols] = mm(low, spread(win[3, :, cols]), TN).astype(BF16)
+
+    for copy in halo[3]:
+        copy.wait_recv()
     cot_cols = jnp.concatenate([cot_basis[i] for i in range(3)], 1)
     pick_cols = one_hot((3 * WIN, WIN), lambda r, c: r == c + start + HALF)
     part = mm_split(mm_split(cot_cols, pick_cols), attn[...]) * GRAD_SCALE + error_left[...]
-    pl.semaphore_wait(barrier, 3 * (LINE - 1) + 1)
     scatter(0, part)
-    cot_halo = [
-        remote(cot_rows.at[pl.ds(0, HALF)], cot_cat.at[pl.ds(HALF + WIN, HALF)], 20, prev_dev),
-        remote(cot_rows.at[pl.ds(HALF, HALF)], cot_cat.at[pl.ds(0, HALF)], 21, next_dev),
-    ]
-    for copy in cot_halo:
-        copy.start()
 
     def send_back(i, arrays, cols):
         copies = [
@@ -253,7 +241,6 @@
 
     load_weight.wait()
     outs[0] = mm(place, mm(attn[...], weight_v[...]).astype(BF16)).astype(BF16)
-    load_cot.wait()
     sum_group(0)
     for copy in cot_halo:
         copy.wait_recv()
@@ -339,29 +326,19 @@
     copies_x, pure_x, forward_x, wait_x, total_x = ring(
         x, lambda to: to * 8 + y_hi * 2 + core, send_x, recv_x, 1, part_x, lambda i: swaps[i].wait_recv()
     )
-    pure_x()
     backward(1)
     backward(2)
     backward(3)
+    pure_x()
     sum_second(0)
+    forward_x()
     back += send_back(18, pl.ds(1, 3), pl.ds(0, WIDTH))
-    forward_x()
-
-    load_error.wait()
+
     left = gathered(0)
-    mine = one_hot((RANK, WIDTH), lambda r, c: c == r + me * RANK)
     left_mine = mm_split(left, mine, NT)
     attn_left = mm_split(left, attn[...], NT)
     part = mm_split(attn_left, cot[...]) * GRAD_SCALE
     scatter(1, part + mm_exact(left_mine, error[...]))
-
-    wait_x()
-    for rows in range(2):
-        mid[2 * rows : 2 * rows + 2] = total_x(rows)
-    copies_y, pure_y, forward_y, wait_y, total_y = ring(
-        y_hi, lambda to: x * 8 + to * 2 + core, send_y, recv_y, 7, part_y, lambda i: None
-    )
-    pure_y()
 
     rows = lax.broadcasted_iota(jnp.int32, (RANK, 1), 0)
     eye = lax.broadcasted_iota(jnp.int32, (RANK, RANK), 0) == lax.broadcasted_iota(jnp.int32, (RANK, RANK), 1)
@@ -375,9 +352,16 @@
     ortho_mine = mm_exact(inverse, left_mine)
 
     sum_group(1)
-    forward_y()
+    wait_x()
+    for rows in range(2):
+        mid[2 * rows : 2 * rows + 2] = total_x(rows)
+    copies_y, pure_y, forward_y, wait_y, total_y = ring(
+        y_hi, lambda to: x * 8 + to * 2 + core, send_y, recv_y, 7, part_y, lambda i: None
+    )
+    pure_y()
     sum_first(1)
     sum_second(1)
+    forward_y()
 
     for copy in back:
         copy.wait_recv()
@@ -397,7 +381,7 @@
 
     for n in range(2):
         sent(n)
-    for copy in [*swaps, *copies_x.values(), *copies_y.values(), *back, *cot_halo]:
+    for copy in [*swaps, *copies_x.values(), *copies_y.values(), *back, *cot_halo, *sum(halo, [])]:
         copy.wait_send()
 
 
@@ -418,40 +402,22 @@
 def body(
     query_rows, key_rows, value_rows, cotangent, out_weight, error_rows, window_shift, basis_seed
 ):
-    error = stay(error_rows[0])
-    cot_rows = stay(cotangent[0])
     smem = pl.BlockSpec(memory_space=pltpu.SMEM)
     vmem = pl.BlockSpec(memory_space=pltpu.VMEM)
     hbm = pl.BlockSpec(memory_space=pltpu.HBM)
     square = jax.ShapeDtypeStruct((RANK, WIDTH), F32)
-    cat, cot_basis, basis, error_left = pl.pallas_call(
-        halo_kernel,
-        out_shape=(
-            jax.ShapeDtypeStruct((3, 2 * WIN, WIDTH), BF16),
-            jax.ShapeDtypeStruct((3, RANK, WIN), F32),
-            square,
-            square,
-        ),
-        in_specs=[smem] + [hbm] * 5,
-        out_specs=(vmem,) * 4,
-        scratch_shapes=[
-            pltpu.VMEM((WIN, WIDTH), BF16),
-            pltpu.VMEM((RANK, WIDTH), F32),
-            pltpu.SemaphoreType.DMA((8,)),
-            pltpu.SemaphoreType.DMA((8,)),
-            pltpu.SemaphoreType.DMA((5,)),
-        ],
-        compiler_params=pltpu.CompilerParams(collective_id=0, has_side_effects=True, vmem_limit_bytes=8 * 2**20),
-        name="halo",
-    )(basis_seed, *(stay(rows[0]) for rows in (query_rows, key_rows, value_rows)), cot_rows, error)
     rows = jax.ShapeDtypeStruct((WIN, WIDTH), BF16)
     results = (rows,) * 4 + (square,) * 3
     parts = pl.pallas_call(
         main_kernel,
         out_shape=results,
-        in_specs=[smem] + [vmem] * 4 + [hbm] * 3,
+        in_specs=[smem] * 2 + [hbm] * 6,
         out_specs=(vmem,) * 7,
         scratch_shapes=[
+            pltpu.VMEM((3, 2 * WIN, WIDTH), BF16),
+            pltpu.VMEM((3, RANK, WIN), F32),
+            pltpu.VMEM((RANK, WIDTH), F32),
+            pltpu.VMEM((RANK, WIDTH), F32),
             pltpu.VMEM((WIDTH, WIDTH), BF16),
             pltpu.VMEM((RANK, WIDTH), F32),
             pltpu.VMEM((2 * WIN, WIDTH), BF16),
@@ -478,13 +444,21 @@
             pltpu.SemaphoreType.DMA((8,)),
             pltpu.SemaphoreType.DMA((22,)),
             pltpu.SemaphoreType.DMA((22,)),
-            pltpu.SemaphoreType.DMA((3,)),
+            pltpu.SemaphoreType.DMA((10,)),
+            pltpu.SemaphoreType.DMA((10,)),
+            pltpu.SemaphoreType.DMA((6,)),
         ],
         compiler_params=pltpu.CompilerParams(
-            collective_id=1, has_side_effects=True, vmem_limit_bytes=32 * 2**20
+            collective_id=0, has_side_effects=True, vmem_limit_bytes=32 * 2**20
         ),
         name="main",
-    )(window_shift, cat, cot_basis, basis, error_left, stay(out_weight), cot_rows, error)
+    )(
+        basis_seed,
+        window_shift,
+        *(stay(a[0]) for a in (query_rows, key_rows, value_rows, cotangent)),
+        stay(out_weight),
+        stay(error_rows[0]),
+    )
     projected, qgrad, kgrad, vgrad, update, new_error, new_basis = pl.pallas_call(
         place_kernel,
         out_shape=results,

time: 75.7 us -> 73.6 us (0.972); the launches traced: 74.3 us -> 73.5 us
  Pallas kernels: 72.4 us -> 71.5 us
    pallas_call x2 -> x1, Pallas kernels: 71.2 us -> 70.4 us  [body(): pl.pallas_call(main_kernel, out_shape=results, in_specs=[smem] * 2 + [hbm...]
where the time goes in v4:
time: 73.6 us; the launch traced here: 73.5 us
  Pallas kernels  71.5 us (97%)
  between operations  1.93 us (3%)
    pallas_call x1, Pallas kernels, body(): pl.pallas_call(main_kernel, out_shape=results, in_specs=[smem] * 2 + [hbm...  70.4 us

profile of v4, /device:TPU:1, one launch (start us, length us, event | category | flops | bytes accessed | tf_op | source)
XLA Modules:
  0.0 73.5 jit_solution(9673512983429228359)
XLA Ops:
  1.9 70.4 %main.1 = (bf16[128,1024]{1,0:T(8,128)(2,1)S(1)}, bf16[128,1024]{1,0:T(8,128)(2,1)S(1)}, bf16[128,1024]{1,0:T(8,128)(2,1)S(1)}, bf16[128,1024]{1,0:T(8,128)(2,1)...) custom-call(s32[1]{0:T(128)S(6)} %copy.16.seed, s32[1]{0:T(128)S(6)} %copy.15.shift, ...), custom_call_target="tpu_custom_call" | custom-call | tf_op jit(solution)/shard_map/main/pallas_call | solution.py:411
  72.3 1.2 %place.1 = (bf16[128,1024]{1,0:T(8,128)(2,1)}, bf16[128,1024]{1,0:T(8,128)(2,1)}, bf16[128,1024]{1,0:T(8,128)(2,1)}, bf16[128,1024]{1,0:T(8,128)(2,1)}, f32[32,1...) custom-call(bf16[128,1024]{1,0:T(8,128)(2,1)S(1)} %get-tuple-element.21.refs_0_, ...), custom_call_target="tpu_custom_call" | custom-call | tf_op jit(solution)/shard_map/place/pallas_call | solution.py:462

commit v5 on v4

--- a/solution.py
+++ b/solution.py
@@ -69,7 +69,7 @@
     seed, shift, query, key, value, cot_rows, weight, error_rows,
     projected, qgrad, kgrad, vgrad, update, new_error, new_basis,
     cat, cot_basis, basis, error_left, weight_v, error, cot_cat, win, dattn, attn, probs_s, outs, grad, grad_low, recv_c, send_x, recv_x, mid, send_y, recv_y,
-    ret_prev, ret_next, chunks, scat, sums, gath,
+    ret_prev, ret_next, chunks, scat, sums, gath, inverse_s, ortho_s,
     send_sem, recv_sem, big_send, big_recv, halo_send, halo_recv, local_sem,
 ):
     me = lax.axis_index("tok")
@@ -340,16 +340,19 @@
     part = mm_split(attn_left, cot[...]) * GRAD_SCALE
     scatter(1, part + mm_exact(left_mine, error[...]))
 
-    rows = lax.broadcasted_iota(jnp.int32, (RANK, 1), 0)
-    eye = lax.broadcasted_iota(jnp.int32, (RANK, RANK), 0) == lax.broadcasted_iota(jnp.int32, (RANK, RANK), 1)
-    gram = mm_exact(left, left, NT)
-    inverse = jnp.where(eye, 1.0, 0.0)
-    for j in range(RANK - 1):
-        factor = jnp.where(rows > j, gram[:, j : j + 1], 0.0) * (1.0 / gram[j : j + 1, j : j + 1])
-        gram, inverse = gram - factor * gram[j : j + 1], inverse - factor * inverse[j : j + 1]
-    pivots = jnp.sum(jnp.where(eye, gram, 0.0), axis=1, keepdims=True)
-    inverse = inverse * (1.0 / jnp.sqrt(pivots))
-    ortho_mine = mm_exact(inverse, left_mine)
+    @pl.when(me >= 0)
+    def _():
+        rows = lax.broadcasted_iota(jnp.int32, (RANK, 1), 0)
+        eye = lax.broadcasted_iota(jnp.int32, (RANK, RANK), 0) == lax.broadcasted_iota(jnp.int32, (RANK, RANK), 1)
+        gram = mm_exact(left, left, NT)
+        inverse = jnp.where(eye, 1.0, 0.0)
+        for j in range(RANK - 1):
+            factor = jnp.where(rows > j, gram[:, j : j + 1], 0.0) * (1.0 / gram[j : j + 1, j : j + 1])
+            gram, inverse = gram - factor * gram[j : j + 1], inverse - factor * inverse[j : j + 1]
+        pivots = jnp.sum(jnp.where(eye, gram, 0.0), axis=1, keepdims=True)
+        inverse = inverse * (1.0 / jnp.sqrt(pivots))
+        ortho_s[...] = mm_exact(inverse, left_mine)
+        inverse_s[...] = inverse
 
     sum_group(1)
     wait_x()
@@ -370,8 +373,8 @@
         out[HALF:WIN] = outs[i, WIN : WIN + HALF] + ret_next[i]
 
     product = gathered(1)
-    basis_t = mm_exact(inverse, product)
-    low_rank = mm_exact(ortho_mine, basis_t, TN)
+    basis_t = mm_exact(inverse_s[...], product)
+    low_rank = mm_exact(ortho_s[...], basis_t, TN)
     update[...] = low_rank
     new_basis[...] = basis_t
     wait_y()
@@ -440,6 +443,8 @@
             pltpu.VMEM((2, LINE, RANK, 128), F32),
             pltpu.VMEM((2, 2, LINE, RANK, 128), F32),
             pltpu.VMEM((2, LINE, RANK, 128), F32),
+            pltpu.VMEM((RANK, RANK), F32),
+            pltpu.VMEM((RANK, RANK), F32),
             pltpu.SemaphoreType.DMA((8,)),
             pltpu.SemaphoreType.DMA((8,)),
             pltpu.SemaphoreType.DMA((22,)),

time: 73.6 us -> 70.9 us (0.963)
  Pallas kernels: 71.5 us -> 68.8 us
    pallas_call x1, Pallas kernels: 70.4 us -> 67.6 us  [body(): pl.pallas_call(main_kernel, out_shape=results, in_specs=[smem] * 2 + [hbm...]
where the time goes in v5:
time: 70.9 us; the launch traced here: 70.7 us
  Pallas kernels  68.8 us (97%)
  between operations  1.93 us (3%)
    pallas_call x1, Pallas kernels, body(): pl.pallas_call(main_kernel, out_shape=results, in_specs=[smem] * 2 + [hbm...  67.6 us

profile of v5, /device:TPU:1, one launch (start us, length us, event | category | flops | bytes accessed | tf_op | source)
XLA Modules:
  0.0 70.7 jit_solution(18200774810572838150)
XLA Ops:
  1.9 67.6 %main.1 = (bf16[128,1024]{1,0:T(8,128)(2,1)S(1)}, bf16[128,1024]{1,0:T(8,128)(2,1)S(1)}, bf16[128,1024]{1,0:T(8,128)(2,1)S(1)}, bf16[128,1024]{1,0:T(8,128)(2,1)...) custom-call(s32[1]{0:T(128)S(6)} %copy.16.seed, s32[1]{0:T(128)S(6)} %copy.15.shift, ...), custom_call_target="tpu_custom_call" | custom-call | tf_op jit(solution)/shard_map/main/pallas_call | solution.py:414
  69.6 1.2 %place.1 = (bf16[128,1024]{1,0:T(8,128)(2,1)}, bf16[128,1024]{1,0:T(8,128)(2,1)}, bf16[128,1024]{1,0:T(8,128)(2,1)}, bf16[128,1024]{1,0:T(8,128)(2,1)}, f32[32,1...) custom-call(bf16[128,1024]{1,0:T(8,128)(2,1)S(1)} %get-tuple-element.21.refs_0_, ...), custom_call_target="tpu_custom_call" | custom-call | tf_op jit(solution)/shard_map/place/pallas_call | solution.py:467

commit v6 on v5

--- a/solution.py
+++ b/solution.py
@@ -240,7 +240,11 @@
         return copies
 
     load_weight.wait()
-    outs[0] = mm(place, mm(attn[...], weight_v[...]).astype(BF16)).astype(BF16)
+
+    @pl.when(me >= 0)
+    def _():
+        outs[0] = mm(place, mm(attn[...], weight_v[...]).astype(BF16)).astype(BF16)
+
     sum_group(0)
     for copy in cot_halo:
         copy.wait_recv()

time: 70.9 us -> 71 us (level)
  no operation moved by 1% of the time
where the time goes in v6:
time: 71 us; the launch traced here: 70.9 us
  Pallas kernels  68.9 us (97%)
  between operations  1.93 us (3%)
    pallas_call x1, Pallas kernels, body(): pl.pallas_call(main_kernel, out_shape=results, in_specs=[smem] * 2 + [hbm...  67.8 us

profile of v6, /device:TPU:1, one launch (start us, length us, event | category | flops | bytes accessed | tf_op | source)
XLA Modules:
  0.0 70.9 jit_solution(2130419748627882376)
XLA Ops:
  1.9 67.8 %main.1 = (bf16[128,1024]{1,0:T(8,128)(2,1)S(1)}, bf16[128,1024]{1,0:T(8,128)(2,1)S(1)}, bf16[128,1024]{1,0:T(8,128)(2,1)S(1)}, bf16[128,1024]{1,0:T(8,128)(2,1)...) custom-call(s32[1]{0:T(128)S(6)} %copy.16.seed, s32[1]{0:T(128)S(6)} %copy.15.shift, ...), custom_call_target="tpu_custom_call" | custom-call | tf_op jit(solution)/shard_map/main/pallas_call | solution.py:418
  69.7 1.2 %place.1 = (bf16[128,1024]{1,0:T(8,128)(2,1)}, bf16[128,1024]{1,0:T(8,128)(2,1)}, bf16[128,1024]{1,0:T(8,128)(2,1)}, bf16[128,1024]{1,0:T(8,128)(2,1)}, f32[32,1...) custom-call(bf16[128,1024]{1,0:T(8,128)(2,1)S(1)} %get-tuple-element.21.refs_0_, ...), custom_call_target="tpu_custom_call" | custom-call | tf_op jit(solution)/shard_map/place/pallas_call | solution.py:471
